TPU v7x, 256 devices: a whole 4x4x8 slice. The times are simulated.
256 devices in a mesh: cb: 4 (over x), tp: 64 (over z, y, core).
Axes of the slice: x: 4, y: 4, z: 8, core: 2. Of those that a mesh axis runs over, the one named last changes fastest.
Arguments:
- hidden_in: bfloat16 [1024, 4096], P('cb', 'tp'), may hold values from -6 to 6
- norm_gain: bfloat16 [4096], P('tp'), may hold values from 0.25 to 1.75
- w_qkv: bfloat16 [3, 4096, 4096], P(None, None, 'tp'), may hold values from -0.0625 to 0.0625
- w_out: bfloat16 [4096, 4096], P('tp'), may hold values from -0.09375 to 0.09375
- cache_keys: bfloat16 [1024, 64, 4096], P(('cb', 'tp')), may hold values from -6 to 6
- cache_values: bfloat16 [1024, 64, 4096], P(('cb', 'tp')), may hold values from -6 to 6
- lengths: int32 [1024], P(('cb', 'tp')), may hold values from 2 to 64, as said below
- tokens: int32 [1024, 8], P(None, 'cb'), may hold values from 0 to 2047
- w_in: bfloat16 [8, 4096, 1024], P('cb', 'tp'), may hold values from -0.09375 to 0.09375
- embed: bfloat16 [8, 2048, 1024], P('cb', None, 'tp'), may hold values from -6 to 6
- depth_gain: bfloat16 [8, 1024], P('cb'), may hold values from 0.25 to 1.75
- w_gate_up: bfloat16 [8, 2, 1024, 2816], P('cb', None, None, 'tp'), may hold values from -0.1875 to 0.1875
- w_down: bfloat16 [8, 2816, 1024], P('cb', 'tp'), may hold values from -0.109375 to 0.109375
Outputs:
- temporal_out: bfloat16 [1024, 4096], P('cb', 'tp')
- depth_out: bfloat16 [8, 1024, 1024], P('cb', None, 'tp')
Inputs may be any that keep to these rules, and one draw needn't show every extreme that they name: `lengths`: number of live cache slots of each stream-beam; some row has all 64.
All inputs are finite; a program needn't handle non-finite values.
Results may differ from a plain program's by a relative error of at most 0.009.
Values may be sent and summed in bfloat16 or wider, within the bound.
No kernel may reach another device: no remote copies, remote signals or barrier semaphores. Data moves between devices by JAX's collectives and lax.ppermute only.
A program may use at most 64 MiB of HBM per device.

v0:
```python
import math

import jax
import jax.numpy as jnp
from jax import lax
from jax.sharding import PartitionSpec as P

D = 4096
HEADS = 32
HEAD_DIM = 128
DD = 1024
CARD = 2048
CACHE = 64


eps = 1e-05


def from_behind(value, axis, steps):
    count = lax.axis_size(axis)
    pairs = [(source, (source + steps) % count) for source in range(count)]
    return lax.ppermute(value, axis, pairs)


def per_device(
    hidden_in,
    norm_gain,
    w_qkv,
    w_out,
    cache_keys,
    cache_values,
    lengths,
    tokens,
    w_in,
    embed,
    depth_gain,
    w_gate_up,
    w_down,
):
    width_tp = lax.axis_size("tp")
    group_rows, feat_loc = hidden_in.shape
    hid32 = hidden_in.astype(jnp.float32)
    sum_sq = lax.psum(jnp.sum(hid32 * hid32, axis=1), "tp")
    normed = (hid32 * lax.rsqrt(sum_sq / D + eps)[:, None] * norm_gain.astype(jnp.float32)).astype(
        jnp.bfloat16
    )
    qkv = jnp.einsum(
        "rd,idf->rif",
        lax.all_gather(normed, "tp", axis=1, tiled=True),
        w_qkv,
        preferred_element_type=jnp.float32,
    ).astype(jnp.bfloat16)
    per_dev = group_rows // width_tp
    arrived = lax.all_to_all(
        qkv.reshape(width_tp, per_dev, 3, feat_loc), "tp", split_axis=0, concat_axis=3, tiled=True
    )
    arrived = arrived.reshape(per_dev, 3, D)
    scale = 1.0 / math.sqrt(HEAD_DIM)
    query_h = arrived[:, 0].reshape(per_dev, HEADS, HEAD_DIM)
    key_new = arrived[:, 1].reshape(per_dev, HEADS, HEAD_DIM)
    value_new = arrived[:, 2].reshape(per_dev, HEADS, HEAD_DIM)
    keys_h = cache_keys.reshape(per_dev, CACHE, HEADS, HEAD_DIM)
    values_h = cache_values.reshape(per_dev, CACHE, HEADS, HEAD_DIM)
    scores = (
        jnp.einsum("rhe,rphe->rhp", query_h, keys_h, preferred_element_type=jnp.float32) * scale
    )
    live = lax.broadcasted_iota(jnp.int32, (1, 1, CACHE), 2) < lengths[:, None, None]
    scores = jnp.where(live, scores, -1e30)
    fresh = jnp.sum(query_h.astype(jnp.float32) * key_new.astype(jnp.float32), axis=-1) * scale
    top = jnp.maximum(jnp.max(scores, axis=-1), fresh)
    weights = jnp.exp(scores - top[..., None])
    weight_new = jnp.exp(fresh - top)
    total = jnp.sum(weights, axis=-1) + weight_new
    probs = (weights / total[..., None]).astype(jnp.bfloat16)
    prob_new = (weight_new / total).astype(jnp.bfloat16)
    mixed = jnp.einsum("rhp,rphe->rhe", probs, values_h, preferred_element_type=jnp.float32)
    mixed = mixed + prob_new.astype(jnp.float32)[..., None] * value_new.astype(jnp.float32)
    attended = mixed.reshape(per_dev, width_tp, feat_loc).astype(jnp.bfloat16)
    returned = lax.all_to_all(attended, "tp", split_axis=1, concat_axis=0, tiled=True).reshape(
        group_rows, feat_loc
    )
    partial_value = jnp.dot(returned, w_out, preferred_element_type=jnp.float32)
    attn_sum = lax.psum_scatter(partial_value, "tp", scatter_dimension=1, tiled=True)
    temporal_out = (hid32 + attn_sum).astype(jnp.bfloat16)
    frame = lax.all_gather(temporal_out, "cb", axis=0, tiled=True)
    steps_here = w_in.shape[0]
    depth_loc = embed.shape[2]
    column_start = lax.axis_index("tp") * depth_loc
    codes = lax.broadcasted_iota(jnp.int32, (1, CARD), 1)
    embedded = []
    for local in range(steps_here):
        one_hot = (tokens[:, local][:, None] == codes).astype(jnp.bfloat16)
        embedded.append(
            jnp.dot(one_hot, embed[local], preferred_element_type=jnp.float32).astype(jnp.bfloat16)
        )
    carried = from_behind(embedded[steps_here - 1], "cb", 1)
    previous = [carried] + embedded[: steps_here - 1]
    results = []
    for local in range(steps_here):
        term = jnp.dot(frame, w_in[local], preferred_element_type=jnp.float32)
        gain_all = depth_gain[local].astype(jnp.float32)
        x_loc = lax.psum_scatter(term, "tp", scatter_dimension=1, tiled=True) + previous[
            local
        ].astype(jnp.float32)
        sum_d = lax.psum(jnp.sum(x_loc * x_loc, axis=1), "tp")
        gain_loc = lax.dynamic_slice_in_dim(gain_all, column_start, depth_loc, 0)
        xn_loc = (x_loc * lax.rsqrt(sum_d / DD + eps)[:, None] * gain_loc).astype(jnp.bfloat16)
        weights_step = w_gate_up[local]
        gate_up = jnp.einsum(
            "rd,idf->irf",
            lax.all_gather(xn_loc, "tp", axis=1, tiled=True),
            weights_step,
            preferred_element_type=jnp.float32,
        )
        act = (jax.nn.silu(gate_up[0]) * gate_up[1]).astype(jnp.bfloat16)
        down_term = jnp.dot(act, w_down[local], preferred_element_type=jnp.float32)
        down_sum = lax.psum_scatter(down_term, "tp", scatter_dimension=1, tiled=True)
        results.append((x_loc + down_sum).astype(jnp.bfloat16))
    return (temporal_out, jnp.stack(results))


def solution(mesh):
    in_specs = (
        P("cb", "tp"),
        P("tp"),
        P(None, None, "tp"),
        P("tp", None),
        P(("cb", "tp"), None, None),
        P(("cb", "tp"), None, None),
        P(("cb", "tp")),
        P(None, "cb"),
        P("cb", "tp", None),
        P("cb", None, "tp"),
        P("cb", None),
        P("cb", None, None, "tp"),
        P("cb", "tp", None),
    )
    out_specs = (P("cb", "tp"), P("cb", None, "tp"))
    return jax.shard_map(
        per_device, mesh=mesh, in_specs=in_specs, out_specs=out_specs, check_vma=False
    )
```

profile of v0, /device:TPU:1, one launch (start us, length us, event | category | flops | bytes accessed | tf_op | source)
XLA Modules:
  0.0 1275.8 jit_solution(14671038319664843020)
XLA Ops:
  8.8 128.3 %psum.21 = f32[256]{0:T(256)S(1)} all-reduce(f32[256]{0:T(256)S(1)} %fusion.38), channel_id=1, replica_groups=mesh['cb'=4,'tp'=64] {'tp'}, use_global_device_ids=true, to_apply=%region_1.0 | all-reduce | flops 256 | bytes 2048 | tf_op jit(solution)/shard_map/psum | solution.py:43
  138.6 76.8 %all-gather.4.cloned.1.call-done = bf16[256,4096]{0,1:T(8,128)(2,1)} async-done(((bf16[256,64]{0,1:T(8,128)(2,1)}), bf16[256,4096]{0,1:T(8,128)(2,1)}) %all-gather.4.cloned.1.call-update) | async-done | bytes 2097168 | tf_op jit(solution)/shard_map/all_gather | solution.py:49
  215.4 2.7 fusion.66
  219.1 6.6 all-to-all-start
  225.9 10.4 all-to-all-done
  237.0 2.8 fusion.7
  241.2 13.1 %all_to_all.30 = bf16[64,2,128]{2,1,0:T(2,128)(2,1)S(1)} all-to-all(bf16[64,2,128]{2,1,0:T(2,128)(2,1)S(1)} %reshape.103), channel_id=1, replica_groups=mesh['cb'=4,'tp'=64] {'tp'}, dimensions={0} | all-to-all | bytes 65536 | tf_op jit(solution)/shard_map/all_to_all | solution.py:79
  254.5 2.7 fusion.65
  257.2 133.5 %reduce-scatter.6.cloned.1.call-done = f32[256,64]{0,1:T(8,128)} async-done(((f32[256,4096]{0,1:T(8,128)}), f32[256,64]{0,1:T(8,128)}) %reduce-scatter.6.cloned.1.call-update) | async-done | bytes 65552 | tf_op jit(solution)/shard_map/reduce_scatter | solution.py:83
  391.6 9.3 all_gather.13
  400.9 2.7 fusion.26
  403.7 2.7 fusion.28
  410.0 138.0 %reduce-scatter.12.cloned.1.call-done = f32[1024,16]{0,1:T(8,128)} async-done(((f32[1024,1024]{0,1:T(8,128)}), f32[1024,16]{0,1:T(8,128)}) %reduce-scatter.12.cloned.1.call-update) | async-done | bytes 65552 | tf_op jit(solution)/shard_map/reduce_scatter | solution.py:102
  547.9 2.5 multiply_reduce_fusion
  550.5 143.6 %reduce-scatter.8.cloned.1.call-done = f32[1024,16]{0,1:T(8,128)} async-done(((f32[1024,1024]{0,1:T(8,128)}), f32[1024,16]{0,1:T(8,128)}) %reduce-scatter.8.cloned.1.call-update) | async-done | bytes 65552 | tf_op jit(solution)/shard_map/reduce_scatter | solution.py:102
  695.0 131.5 %all-reduce = (f32[1024]{0:T(1024)S(1)}, f32[1024]{0:T(1024)S(1)}) all-reduce(f32[1024]{0:T(1024)S(1)} %get-tuple-element.18, f32[1024]{0:T(1024)S(1)} %multiply_reduce_fusion.1), channel_id=1, replica_groups=mesh['cb'=4,'tp'=64] {'tp'}, use_global_device_ids=true, to_apply=%region_12.13 | all-reduce | flops 2048 | bytes 16384 | tf_op jit(solution)/shard_map/psum | solution.py:105
  829.7 72.7 %all-gather.8.cloned.1.call-done = bf16[1024,1024]{0,1:T(8,128)(2,1)} async-done(((bf16[1024,16]{0,1:T(8,128)(2,1)}), bf16[1024,1024]{0,1:T(8,128)(2,1)}) %all-gather.8.cloned.1.call-update) | async-done | bytes 2097168 | tf_op jit(solution)/shard_map/all_gather | solution.py:111
  902.5 2.1 fusion.17
  904.5 2.7 fusion.32
  907.3 73.2 %all-gather.6.cloned.1.call-done = bf16[1024,1024]{0,1:T(8,128)(2,1)} async-done(((bf16[1024,16]{0,1:T(8,128)(2,1)}), bf16[1024,1024]{0,1:T(8,128)(2,1)}) %all-gather.6.cloned.1.call-update) | async-done | bytes 2097168 | tf_op jit(solution)/shard_map/all_gather | solution.py:111
  980.4 2.1 fusion.14
  982.5 2.7 fusion.33
  985.3 135.9 %reduce-scatter.14.cloned.1.call-done = f32[1024,16]{0,1:T(8,128)} async-done(((f32[1024,1024]{0,1:T(8,128)}), f32[1024,16]{0,1:T(8,128)}) %reduce-scatter.14.cloned.1.call-update) | async-done | bytes 65552 | tf_op jit(solution)/shard_map/reduce_scatter | solution.py:117
  1122.0 145.4 %reduce-scatter.10.cloned.1.call-done = f32[1024,16]{0,1:T(8,128)} async-done(((f32[1024,1024]{0,1:T(8,128)}), f32[1024,16]{0,1:T(8,128)}) %reduce-scatter.10.cloned.1.call-update) | async-done | bytes 65552 | tf_op jit(solution)/shard_map/reduce_scatter | solution.py:117
  (85 shorter events, 17.4 us)
Async XLA Ops:
  7.2 233.1 %copy-start = (bf16[4,64,4096]{2,1,0:T(8,128)(2,1)S(1)}, bf16[4,64,4096]{2,1,0:T(8,128)(2,1)}, u32[]{:S(2)}) copy-start(bf16[4,64,4096]{2,1,0:T(8,128)(2,1)} %param.18) | copy-start | bytes 6291460
  7.2 208.2 %all-gather.4.cloned.1.call-start = ((), (), s32[]{:S(2)}) async-start(), calls=%async_computation.7 | async-start | bytes 2129920 | tf_op jit(solution)/shard_map/all_gather | solution.py:49
  215.4 10.4 copy-start.11
  219.1 17.2 %all-to-all-start = ((bf16[64,2,384]{2,1,0:T(2,128)(2,1)}), bf16[64,2,384]{2,1,0:T(2,128)(2,1)S(1)}, u32[]{:S(2)}, u32[]{:S(2)}) async-start(bf16[64,2,384]{2,1,0:T(2,128)(2,1)} %reshape.101), calls=%async_computation | async-start | bytes 196608 | tf_op jit(solution)/shard_map/all_to_all | solution.py:54
  225.8 164.9 %reduce-scatter.6.cloned.1.call-start = ((), (), s32[]{:S(2)}) async-start(), calls=%async_computation.8 | async-start | bytes 4259840 | tf_op jit(solution)/shard_map/reduce_scatter | solution.py:83
  239.8 14.7 %copy-start.3 = (bf16[64,4096]{1,0:T(8,128)(2,1)S(1)}, bf16[64,4096]{1,0:T(8,128)(2,1)}, u32[]{:S(2)}) copy-start(bf16[64,4096]{1,0:T(8,128)(2,1)} %param.16) | copy-start | bytes 1572868
  257.2 133.6 %copy-start.5 = (bf16[256,64]{0,1:T(8,128)(2,1)S(1)}, bf16[256,64]{0,1:T(8,128)(2,1)}, u32[]{:S(2)}) copy-start(bf16[256,64]{0,1:T(8,128)(2,1)} %param.13) | copy-start | bytes 98308
  257.2 143.7 %copy-start.6 = (bf16[2,64,1024]{2,1,0:T(8,128)(2,1)S(1)}, bf16[2,64,1024]{2,1,0:T(8,128)(2,1)}, u32[]{:S(2)}) copy-start(bf16[2,64,1024]{2,1,0:T(8,128)(2,1)} %param.21) | copy-start | bytes 786436
  257.2 290.8 %reduce-scatter.12.cloned.1.call-start = ((), (), s32[]{:S(2)}) async-start(), calls=%async_computation.12 | async-start | bytes 4259840 | tf_op jit(solution)/shard_map/reduce_scatter | solution.py:102
  391.6 12.0 copy-start.7
  403.6 290.5 %reduce-scatter.8.cloned.1.call-start = ((), (), s32[]{:S(2)}) async-start(), calls=%async_computation.9 | async-start | bytes 4259840 | tf_op jit(solution)/shard_map/reduce_scatter | solution.py:102
  406.4 0.7 copy-start.9
  406.4 0.9 copy-start.10
  406.4 3.5 copy-start.8
  406.4 496.0 %all-gather.8.cloned.1.call-start = ((), (), s32[]{:S(2)}) async-start(), calls=%async_computation.13 | async-start | bytes 2129920 | tf_op jit(solution)/shard_map/all_gather | solution.py:111
  408.9 141.6 %collective-permute-start = (bf16[1024,16]{0,1:T(8,128)(2,1)S(1)}, bf16[1024,16]{0,1:T(8,128)(2,1)S(1)}, u32[]{:S(2)}, u32[]{:S(2)}) collective-permute-start(bf16[1024,16]{0,1:T(8,128)(2,1)S(1)} %fusion.23), channel_id=1, source_target_pairs={{0,64},{64,128},{128,192},{192,0},{1,65},{65,129},{129,193},{193,1... | collective-permute-start | bytes 98312 | tf_op jit(solution)/shard_map/ppermute | solution.py:22
  547.9 281.2 %copy-start.1 = (bf16[2,44,1024]{2,0,1:T(2,128)(2,1)S(1)}, bf16[2,44,1024]{2,0,1:T(2,128)(2,1)}, u32[]{:S(2)}) copy-start(bf16[2,44,1024]{2,0,1:T(2,128)(2,1)} %param.25) | copy-start | bytes 540676
  547.9 281.5 %copy-start.4 = (bf16[2,2,1024,44]{2,1,3,0:T(2,128)(2,1)S(1)}, bf16[2,2,1024,44]{2,1,3,0:T(2,128)(2,1)}, u32[]{:S(2)}) copy-start(bf16[2,2,1024,44]{2,1,3,0:T(2,128)(2,1)} %param.24) | copy-start | bytes 1081348
  827.3 153.2 %all-gather.6.cloned.1.call-start = ((), (), s32[]{:S(2)}) async-start(), calls=%async_computation.10 | async-start | bytes 2129920 | tf_op jit(solution)/shard_map/all_gather | solution.py:111
  829.0 292.2 %reduce-scatter.14.cloned.1.call-start = ((), (), s32[]{:S(2)}) async-start(), calls=%async_computation.14 | async-start | bytes 4259840 | tf_op jit(solution)/shard_map/reduce_scatter | solution.py:117
  907.2 360.2 %reduce-scatter.10.cloned.1.call-start = ((), (), s32[]{:S(2)}) async-start(), calls=%async_computation.11 | async-start | bytes 4259840 | tf_op jit(solution)/shard_map/reduce_scatter | solution.py:117
  985.2 282.2 %copy-start.2 = (f32[1024,16]{0,1:T(8,128)S(1)}, f32[1024,16]{0,1:T(8,128)}, u32[]{:S(2)}) copy-start(f32[1024,16]{0,1:T(8,128)} %reduce-scatter.8.cloned.1.call-done) | copy-start | bytes 196612
Sparse Core Ops, SparseCore 0:
  138.7 76.6 all-gather.3
  257.3 133.3 reduce-scatter.5
  403.7 144.1 reduce-scatter.11
  551.9 142.1 reduce-scatter.7
  827.4 75.0 all-gather.7
  905.5 74.9 all-gather.5
  985.1 135.9 reduce-scatter.13
  1125.3 142.1 reduce-scatter.9
where the time goes:
time: 1280 us
  waiting for transfers between devices  930 us (73%)
  blocking collectives  282 us (22%)
  matrix products  27.9 us (2%)
  between operations  14.4 us (1%)
    reduce_scatter x2, waiting for transfers between devices, per_device(): lax.psum_scatter(term, 'tp', scatter_dimension=1, tiled=True)  282 us
    reduce_scatter x2, waiting for transfers between devices, per_device(): lax.psum_scatter(down_term, 'tp', scatter_dimension=1, tiled=True)  281 us
    all_gather x2, waiting for transfers between devices, per_device(): lax.all_gather(xn_loc, 'tp', axis=1, tiled=True)  146 us
    reduce_scatter x1, waiting for transfers between devices, per_device(): lax.psum_scatter(partial_value, 'tp', scatter_dimension=1, tiled=True)  133 us
    psum x1, blocking collectives, per_device(): sum_d = lax.psum(jnp.sum(x_loc * x_loc, axis=1), 'tp')  132 us
    psum x1, blocking collectives, per_device(): sum_sq = lax.psum(jnp.sum(hid32 * hid32, axis=1), 'tp')  128 us
    all_gather x1, waiting for transfers between devices, per_device(): lax.all_gather(normed, 'tp', axis=1, tiled=True)  76.8 us
  transfers between devices with their start and end apart: 10, of which 9 were waited for; matrix products, arithmetic and copies ran while one was open for 2% of the time, Pallas kernels for 0%

commit v1 on v0

v1 whole, which is shorter than its diff:
```python
import math

import jax
import jax.numpy as jnp
from jax import lax
from jax.sharding import Mesh, PartitionSpec as P

D = 4096
HEADS = 32
HEAD_DIM = 128
DD = 1024
CARD = 2048
CACHE = 64
X, Z, Y, C = 4, 8, 4, 2
HID = 44
HID_PAD = 96

eps = 1e-05
BF = jnp.bfloat16
F32 = jnp.float32
TP = ("z", "y", "core")


def exchange(value, axis):
    return lax.all_to_all(value, axis, split_axis=0, concat_axis=0, tiled=True)


def spread(value, axis):
    count = lax.axis_size(axis)
    copies = jnp.broadcast_to(value[None], (count,) + value.shape)
    return exchange(copies, axis)


def swap(value):
    return lax.ppermute(value, "core", [(0, 1), (1, 0)])


def pick(value, index):
    return lax.dynamic_index_in_dim(value, index, 0, keepdims=False)


def per_device(
    hidden_in,
    norm_gain,
    w_qkv,
    w_out,
    cache_keys,
    cache_values,
    lengths,
    tokens,
    w_in,
    embed,
    depth_gain,
    w_gate_up,
    w_down,
):
    xi, zi, yi, ci = (lax.axis_index(a) for a in ("cb", "z", "y", "core"))
    other = 1 - ci

    with jax.named_scope("pack_weights"):
        emb_t = embed.transpose(0, 2, 1)
        emb_r = jnp.concatenate([emb_t[:, :, :DD], emb_t[:, :, DD:]], axis=1)
        keep_a = jnp.concatenate([pick(w_in, ci), pick(emb_r, other)], axis=0)
        send_a = jnp.concatenate([pick(w_in, other), pick(emb_r, ci)], axis=0)
        recv_a = swap(send_a)
        wo = lax.dynamic_slice_in_dim(w_out, xi * DD, DD, 1)
        wo = wo.reshape(64, 2, 8, 64).transpose(0, 2, 1, 3).reshape(64, DD)
        first = lax.all_gather(jnp.concatenate([wo, keep_a, recv_a], axis=0), "z")
        gu_t = w_gate_up.transpose(0, 3, 1, 2)
        own_gu, own_dn = pick(gu_t, ci), pick(w_down, ci)
        send_b = jnp.concatenate(
            [pick(gu_t, other)[:, 0], pick(gu_t, other)[:, 1], pick(w_down, other)], axis=0
        )
        recv_b = swap(send_b)
        fill = jnp.zeros((HID_PAD - 2 * HID, DD), BF)
        second = lax.all_gather(
            jnp.concatenate(
                [
                    own_gu[:, 0],
                    recv_b[:HID],
                    fill,
                    own_gu[:, 1],
                    recv_b[HID : 2 * HID],
                    fill,
                    own_dn,
                    recv_b[2 * HID :],
                    fill,
                ],
                axis=0,
            ),
            "z",
        )

    with jax.named_scope("gather_hidden"):
        gain_row = jnp.pad(norm_gain[None, :], ((0, 7), (0, 192)))
        shard = jnp.concatenate([hidden_in.T, gain_row], axis=0)
        mine = spread(spread(shard, "z"), "y")
        theirs = swap(mine)
        core0 = jnp.where(ci == 0, mine, theirs)
        core1 = jnp.where(ci == 0, theirs, mine)
        both = jnp.stack([core0, core1], axis=0).transpose(2, 1, 0, 3, 4)
        hid = both[:, :, :, :64, :].astype(F32)
        gain = both[:, :, :, 64, :64].astype(F32)
        sum_sq = jnp.sum(hid * hid, axis=(0, 1, 2, 3))
        normed = (hid * lax.rsqrt(sum_sq / D + eps) * gain[..., None]).astype(BF)
        normed = normed.reshape(D, 256)

    with jax.named_scope("qkv"):
        qkv = jnp.einsum("dr,idf->rif", normed, w_qkv, preferred_element_type=F32).astype(BF)
        sent = jnp.concatenate([qkv.reshape(256, 192), hidden_in], axis=1)
        got = exchange(sent.reshape(64, 4, 256), TP)
        got = got.reshape(HEADS, 2, 4, 4, 64).transpose(2, 3, 0, 1, 4)
        got = got.reshape(4, 4, HEADS, HEAD_DIM)

    with jax.named_scope("attend"):
        query_h, key_new, value_new = got[:, 0], got[:, 1], got[:, 2]
        hid_rows = got[:, 3]
        scale = 1.0 / math.sqrt(HEAD_DIM)
        keys_h = cache_keys.reshape(4, CACHE, HEADS, HEAD_DIM)
        values_h = cache_values.reshape(4, CACHE, HEADS, HEAD_DIM)
        scores = jnp.einsum("rhe,rphe->rhp", query_h, keys_h, preferred_element_type=F32) * scale
        live = lax.broadcasted_iota(jnp.int32, (1, 1, CACHE), 2) < lengths[:, None, None]
        scores = jnp.where(live, scores, -1e30)
        fresh = jnp.sum(query_h.astype(F32) * key_new.astype(F32), axis=-1) * scale
        top = jnp.maximum(jnp.max(scores, axis=-1), fresh)
        weights = jnp.exp(scores - top[..., None])
        weight_new = jnp.exp(fresh - top)
        total = jnp.sum(weights, axis=-1) + weight_new
        probs = (weights / total[..., None]).astype(BF)
        prob_new = (weight_new / total).astype(BF)
        mixed = jnp.einsum("rhp,rphe->rhe", probs, values_h, preferred_element_type=F32)
        mixed = mixed + prob_new.astype(F32)[..., None] * value_new.astype(F32)
        attended = mixed.astype(BF)

    with jax.named_scope("project"):
        att = attended.reshape(4, Z, Y, C, 64).transpose(2, 3, 0, 1, 4).reshape(1, 8, 4, 512)
        att = jnp.broadcast_to(att, (X, 8, 4, 512))
        res = hid_rows.reshape(4, X, 2, Y, C, 64).transpose(1, 3, 4, 0, 2, 5)
        res = res.reshape(X, 8, 4, 128)
        moved = exchange(
            jnp.concatenate([att, res], axis=-1).reshape(32, 4, 640), ("cb", "y", "core")
        ).reshape(128, 640)
        wo_rows = first[:, :64].reshape(512, DD)
        part = jnp.dot(moved[:, :512], wo_rows, preferred_element_type=F32).astype(BF)
        part = exchange(part.reshape(128, 8, 128).transpose(1, 0, 2), ("y", "core"))
        temporal = jnp.sum(part.astype(F32), axis=0) + moved[:, 512:].astype(F32)
        temporal = temporal.astype(BF)
        frame = spread(temporal, "cb")
        frame_all = jnp.concatenate([frame, swap(frame)], axis=0)

    with jax.named_scope("embed"):
        token = lax.dynamic_index_in_dim(tokens, other, 1, keepdims=False)
        token = lax.dynamic_index_in_dim(token.reshape(X, Z, 32), zi, 1, keepdims=False)
        codes = lax.broadcasted_iota(jnp.int32, (2, DD, 1), 1) + DD * lax.broadcasted_iota(
            jnp.int32, (2, DD, 1), 0
        )
        one_hot = (codes == token.reshape(1, 1, 128)).astype(BF)
        tables = jnp.stack([first[:, 128:160], first[:, 224:256]], axis=0)
        tables = tables.reshape(2, Z, 2, 16, DD)
        emb = jnp.einsum("czhft,htr->czfr", tables, one_hot, preferred_element_type=F32)
        emb = emb.astype(BF)
        moved_emb = lax.ppermute(
            emb, ("cb", "core"), [(2 * x, 2 * ((x + 1) % X)) for x in range(X)]
        )
        emb = jnp.where(ci == 0, moved_emb, emb)
        emb0 = jnp.where(ci == 0, emb[0], emb[1])
        emb1 = jnp.where(ci == 0, emb[1], emb[0])
        emb = jnp.stack([emb0, emb1], axis=1)[:, None]
        here = lax.broadcasted_iota(jnp.int32, (1, Y, 1, 1, 1), 1) == yi
        emb = jnp.where(here, emb, jnp.zeros((), BF)).reshape(DD, 128)

    with jax.named_scope("depth_in"):
        win = jnp.concatenate([first[:, 64:128], first[:, 160:224]], axis=0)
        win = win.reshape(8, 128, DD)
        x_part = jnp.einsum("brk,bkn->nr", frame_all, win, preferred_element_type=F32)
        x_part = (x_part + emb.astype(F32)).astype(BF)
        x = jnp.sum(spread(x_part, "y").astype(F32), axis=0)

    with jax.named_scope("depth_ff"):
        mean = jnp.sum(x * x, axis=0) / DD
        gain_d = pick(depth_gain, ci).astype(F32)
        xn = (x * lax.rsqrt(mean + eps) * gain_d[:, None]).astype(BF)
        gate = jnp.einsum(
            "zhd,dr->zhr", second[:, :HID_PAD], xn, preferred_element_type=F32
        )
        upper = jnp.einsum(
            "zhd,dr->zhr", second[:, HID_PAD : 2 * HID_PAD], xn, preferred_element_type=F32
        )
        act = (jax.nn.silu(gate) * upper).astype(BF)
        down = jnp.einsum(
            "zhn,zhr->nr", second[:, 2 * HID_PAD :], act, preferred_element_type=F32
        )
        out = (down + x * (1.0 / Y)).astype(BF)
        out = exchange(out.reshape(Z, Y, 32, 128).transpose(1, 0, 2, 3), "y")
        out = jnp.sum(out.astype(F32), axis=0).astype(BF).reshape(Z, C, 16, 128)

    with jax.named_scope("place_outputs"):
        rows = lax.dynamic_slice_in_dim(frame, xi * 32, 32, 1)
        rows = rows.reshape(X, 2, 16, 2, 64).transpose(0, 3, 2, 1, 4).reshape(Z, 1, 16, 128)
        same = lax.broadcasted_iota(jnp.int32, (1, C, 1, 1), 1) == ci
        rows = jnp.where(same, rows, jnp.zeros((), BF))
        last = exchange(jnp.concatenate([out, rows], axis=2).reshape(16, 32, 128), ("z", "core"))
        last = last.reshape(Z, C, 32, 128)
        depth_out = last[:, :, :16].reshape(Z, C, 16, X, 32).transpose(1, 3, 0, 4, 2)
        depth_out = depth_out.reshape(C, 1024, 16)
        temporal_out = lax.dynamic_index_in_dim(last[:, :, 16:], ci, 1, keepdims=False)
        temporal_out = temporal_out.reshape(Z, 16, 2, 64).transpose(0, 2, 1, 3).reshape(256, 64)
    return (temporal_out, depth_out)


def solution(mesh):
    fine = Mesh(mesh.devices.reshape(X, Z, Y, C), ("cb", "z", "y", "core"))
    every = ("cb",) + TP
    in_specs = (
        P("cb", TP),
        P(TP),
        P(None, None, TP),
        P(TP, None),
        P(every, None, None),
        P(every, None, None),
        P(every),
        P(None, "cb"),
        P("cb", TP, None),
        P("cb", None, TP),
        P("cb", None),
        P("cb", None, None, TP),
        P("cb", TP, None),
    )
    out_specs = (P("cb", TP), P("cb", None, TP))
    return jax.shard_map(
        per_device, mesh=fine, in_specs=in_specs, out_specs=out_specs, check_vma=False
    )
```

time: 1280 us -> 210 us (0.16)
  waiting for transfers between devices: 930 us -> 60.3 us
  blocking collectives: 282 us -> 33.1 us
  local copies, waits for them, and re-layouts: 3.29 us -> 38.5 us
  starting transfers between devices: 8.09 us -> 37.7 us
  matrix products: 27.9 us -> 14 us
    reduce_scatter x5 -> x0, waiting for transfers between devices: 696 us -> none  [the longest x2 282 us: per_device(): lax.psum_scatter(term, 'tp', scatter_dimension=1, tiled=True)]
    psum x2 -> x0, blocking collectives: 260 us -> none  [the longest x1 132 us: per_device(): sum_d = lax.psum(jnp.sum(x_loc * x_loc, axis=1), 'tp')]
    all_gather x3 -> x2, waiting for transfers between devices: 223 us -> 0.04 us  [the longest x1 0.02 us: per_device(): lax.all_gather(jnp.concatenate([own_gu[:, 0], recv_b[:HID], fill, own_gu[...]
    all_to_all x1 -> x7, waiting for transfers between devices: 10.4 us -> 59.5 us  [exchange(): return lax.all_to_all(value, axis, split_axis=0, concat_axis=0, tiled=True)]
    all_to_all x1 -> x7, starting transfers between devices: 6.63 us -> 29 us  [exchange(): return lax.all_to_all(value, axis, split_axis=0, concat_axis=0, tiled=True)]
    all_to_all x1 -> x2, blocking collectives: 13.1 us -> 33.1 us  [exchange(): return lax.all_to_all(value, axis, split_axis=0, concat_axis=0, tiled=True)]
  transfers between devices with their start and end apart: 10 -> 14, of which waited for: 9 -> 8; matrix products, arithmetic and copies ran while one was open for 2% -> 23% of each run, Pallas kernels for 0% -> 0%
where the time goes in v1:
time: 210 us; the launch traced here: 209 us
  waiting for transfers between devices  60.3 us (29%)
  local copies, waits for them, and re-layouts  38.5 us (18%)
  starting transfers between devices  37.7 us (18%)
  blocking collectives  33.1 us (16%)
  between operations  14.7 us (7%)
  matrix products  14 us (7%)
  other arithmetic  10.4 us (5%)
    all_to_all x7, waiting for transfers between devices, exchange(): return lax.all_to_all(value, axis, split_axis=0, concat_axis=0, tiled=True)  59.5 us
    all_to_all x2, blocking collectives, exchange(): return lax.all_to_all(value, axis, split_axis=0, concat_axis=0, tiled=True)  33.1 us
    all_to_all x7, starting transfers between devices, exchange(): return lax.all_to_all(value, axis, split_axis=0, concat_axis=0, tiled=True)  29 us
    concatenate x1, local copies, waits for them, and re-layouts, per_device(): jnp.concatenate([own_gu[:, 0], recv_b[:HID], fill, own_gu[:, 1], recv_b[H...  10.9 us
    ppermute x4, starting transfers between devices, swap(): return lax.ppermute(value, 'core', [(0, 1), (1, 0)])  7.72 us
    unnamed x34, local copies, waits for them, and re-layouts  4.74 us
  transfers between devices with their start and end apart: 14, of which 8 were waited for; matrix products, arithmetic and copies ran while one was open for 23% of the time, Pallas kernels for 0%

profile of v1, /device:TPU:1, one launch (start us, length us, event | category | flops | bytes accessed | tf_op | source)
XLA Modules:
  0.0 208.7 jit_solution(14657957609436163448)
XLA Ops:
  9.3 3.3 %collective-permute-start.1 = (bf16[96,1024]{1,0:T(8,128)(2,1)S(1)}, bf16[96,1024]{1,0:T(8,128)(2,1)S(1)}, u32[]{:S(2)}, u32[]{:S(2)}) collective-permute-start(bf16[96,1024]{1,0:T(8,128)(2,1)S(1)} %pad_maximum_fusion.3), channel_id=1, source_target_pairs={{0,1},{1,0},{2,3},{3,2},{4,5},{5,4},{6,7},{7,6},{8,9},{9,8},{10,11... | collective-permute-start | bytes 589832 | tf_op jit(solution)/shard_map/pack_weights/ppermute | solution.py:35
  15.1 18.9 %all_to_all.45 = bf16[8,72,256]{2,1,0:T(8,128)(2,1)S(1)} all-to-all(bf16[8,72,256]{2,1,0:T(8,128)(2,1)S(1)} %broadcast_in_dim.115), channel_id=1, replica_groups=mesh['cb'=4,'z'=8,'y'=4,'core'=2] {'z'}, dimensions={0} | all-to-all | bytes 589824 | tf_op jit(solution)/shard_map/gather_hidden/all_to_all | solution.py:25
  35.1 4.3 %all-to-all-start.1 = ((bf16[4,8,72,256]{3,2,1,0:T(8,128)(2,1)}), bf16[4,8,72,256]{3,2,1,0:T(8,128)(2,1)S(1)}, u32[]{:S(2)}, u32[]{:S(2)}) async-start(bf16[4,8,72,256]{3,2,1,0:T(8,128)(2,1)} %broadcast_in_dim.116), calls=%async_computation.1 | async-start | bytes 2359296 | tf_op jit(solution)/shard_map/gather_hidden/all_to_all | solution.py:25
  41.4 13.2 %all-to-all-done.1 = bf16[4,8,72,256]{3,2,1,0:T(8,128)(2,1)S(1)} async-done(((bf16[4,8,72,256]{3,2,1,0:T(8,128)(2,1)}), bf16[4,8,72,256]{3,2,1,0:T(8,128)(2,1)S(1)}, u32[]{:S(2)}, u32[]{:S(2)}) %all-to-all-start.1) | async-done | bytes 1179680 | tf_op jit(solution)/shard_map/gather_hidden/all_to_all | solution.py:25
  55.7 2.2 %collective-permute-start.2 = (bf16[4,8,72,256]{3,2,0,1:T(8,128)(2,1)}, bf16[4,8,72,256]{3,2,0,1:T(8,128)(2,1)}, u32[]{:S(2)}, u32[]{:S(2)}) collective-permute-start(bf16[4,8,72,256]{3,2,0,1:T(8,128)(2,1)} %copy.105), channel_id=1, source_target_pairs={{0,1},{1,0},{2,3},{3,2},{4,5},{5,4},{6,7},{7,6},{8,9},{9,8},{10,11... | collective-permute-start | bytes 3538952 | tf_op jit(solution)/shard_map/gather_hidden/ppermute | solution.py:35
  65.2 10.9 %concatenate.48 = bf16[288,1024]{1,0:T(8,128)(2,1)} concatenate(bf16[44,1024]{1,0:T(8,128)(2,1)} %get-tuple-element.27, bf16[44,1024]{1,0:T(8,128)(2,1)} %get-tuple-element.23, bf16[8,1024]{1,0:T(8,128)(2,1)S(1)} %broadcast_in_dim.112, bf16[44,1024]{1,0:T(8,128)(2,1)} %get-tuple-element.26, bf16[44,1024]{1,0:T(8,128)(2,1)S(1)} %get-tuple-element.22, ...), dimensions={0} | concatenate | bytes 1179648 | tf_op jit(solution)/shard_map/pack_weights/concatenate | solution.py:77
  81.5 4.6 %all-to-all-start.2 = ((bf16[64,4,256]{2,1,0:T(4,128)(2,1)}), bf16[64,4,256]{2,1,0:T(4,128)(2,1)S(1)}, u32[]{:S(2)}, u32[]{:S(2)}) async-start(bf16[64,4,256]{2,1,0:T(4,128)(2,1)} %pad_maximum_fusion.5), calls=%async_computation.2 | async-start | bytes 262144 | tf_op jit(solution)/shard_map/qkv/all_to_all | solution.py:25
  86.6 11.9 %all-to-all-done.2 = bf16[64,4,256]{2,1,0:T(4,128)(2,1)S(1)} async-done(((bf16[64,4,256]{2,1,0:T(4,128)(2,1)}), bf16[64,4,256]{2,1,0:T(4,128)(2,1)S(1)}, u32[]{:S(2)}, u32[]{:S(2)}) %all-to-all-start.2) | async-done | bytes 131104 | tf_op jit(solution)/shard_map/qkv/all_to_all | solution.py:25
  99.1 2.8 %fusion.6 = f32[4,32,1,64]{3,2,1,0:T(1,128)S(1)} fusion(bf16[4,32,128,1]{2,1,0,3:T(8,128)(2,1)S(1)} %get-tuple-element.34, bf16[4,64,4096]{2,1,0:T(8,128)(2,1)} %param.17), kind=kOutput, calls=%fused_computation.9 | convolution fusion | flops 2097152 | bytes 2162688 | tf_op jit(solution)/shard_map/attend/rhe,rphe->rhp/dot_general | solution.py:121
  104.4 6.1 %all-to-all-start.3 = ((bf16[32,4,640]{2,1,0:T(4,128)(2,1)}), bf16[32,4,640]{2,1,0:T(4,128)(2,1)S(1)}, u32[]{:S(2)}, u32[]{:S(2)}) async-start(bf16[32,4,640]{2,1,0:T(4,128)(2,1)} %pad_maximum_fusion.4), calls=%async_computation.3 | async-start | bytes 327680 | tf_op jit(solution)/shard_map/project/all_to_all | solution.py:25
  110.5 7.9 %all-to-all-done.3 = bf16[32,4,640]{2,1,0:T(4,128)(2,1)S(1)} async-done(((bf16[32,4,640]{2,1,0:T(4,128)(2,1)}), bf16[32,4,640]{2,1,0:T(4,128)(2,1)S(1)}, u32[]{:S(2)}, u32[]{:S(2)}) %all-to-all-start.3) | async-done | bytes 163872 | tf_op jit(solution)/shard_map/project/all_to_all | solution.py:25
  118.5 3.3 %fusion.84 = (bf16[8,64,1024]{2,1,0:T(8,128)(2,1)S(1)}, bf16[8,64,1024]{2,1,0:T(8,128)(2,1)S(1)}, bf16[8,64,1024]{2,1,0:T(8,128)(2,1)}) fusion(bf16[8,256,1024]{2,1,0:T(8,128)(2,1)} %bitcast.169), kind=kLoop, calls=%fused_computation.140 | loop fusion | bytes 6291456 | tf_op jit(solution)/shard_map/depth_in/slice | solution.py:173
  123.0 3.6 %all-to-all-start.4 = ((bf16[8,128,128]{2,1,0:T(8,128)(2,1)}), bf16[8,128,128]{2,1,0:T(8,128)(2,1)S(1)}, u32[]{:S(2)}, u32[]{:S(2)}) async-start(bf16[8,128,128]{2,1,0:T(8,128)(2,1)} %bitcast.176), calls=%async_computation.4 | async-start | bytes 524288 | tf_op jit(solution)/shard_map/project/all_to_all | solution.py:25
  131.0 2.2 %all-to-all-done.4 = bf16[8,128,128]{2,1,0:T(8,128)(2,1)S(1)} async-done(((bf16[8,128,128]{2,1,0:T(8,128)(2,1)}), bf16[8,128,128]{2,1,0:T(8,128)(2,1)S(1)}, u32[]{:S(2)}, u32[]{:S(2)}) %all-to-all-start.4) | async-done | bytes 262176 | tf_op jit(solution)/shard_map/project/all_to_all | solution.py:25
  134.7 3.3 %all-to-all-start.5 = ((bf16[4,128,128]{2,1,0:T(8,128)(2,1)}), bf16[4,128,128]{2,1,0:T(8,128)(2,1)S(1)}, u32[]{:S(2)}, u32[]{:S(2)}) async-start(bf16[4,128,128]{2,1,0:T(8,128)(2,1)} %broadcast_in_dim.120), calls=%async_computation.5 | async-start | bytes 262144 | tf_op jit(solution)/shard_map/project/all_to_all | solution.py:25
  138.0 4.8 %all-to-all-done.5 = bf16[4,128,128]{2,1,0:T(8,128)(2,1)S(1)} async-done(((bf16[4,128,128]{2,1,0:T(8,128)(2,1)}), bf16[4,128,128]{2,1,0:T(8,128)(2,1)S(1)}, u32[]{:S(2)}, u32[]{:S(2)}) %all-to-all-start.5) | async-done | bytes 131104 | tf_op jit(solution)/shard_map/project/all_to_all | solution.py:25
  145.9 2.3 %fusion.25 = bf16[1024,128]{1,0:T(8,128)(2,1)S(1)} fusion(bf16[8,128,1024]{2,1,0:T(8,128)(2,1)} %bitcast.173, bf16[1024,128]{1,0:T(8,128)(2,1)S(1)} %bitcast_select_fusion, bf16[4,128,128]{2,1,0:T(8,128)(2,1)S(1)} %collective-permute-done.3, bf16[4,128,128]{2,1,0:T(8,128)(2,1)S(1)} %all-to-all-done.5), kind=kOutput, calls=%fused_computation.26 | convolution fusion | flops 268959744 | bytes 2883584 | tf_op jit(solution)/shard_map/depth_in/brk,bkn->nr/dot_general | solution.py:175
  149.4 3.8 %all-to-all-start.6 = ((bf16[4,1024,128]{2,1,0:T(8,128)(2,1)}), bf16[4,1024,128]{2,1,0:T(8,128)(2,1)S(1)}, u32[]{:S(2)}, u32[]{:S(2)}) async-start(bf16[4,1024,128]{2,1,0:T(8,128)(2,1)} %broadcast_in_dim.127), calls=%async_computation.6 | async-start | bytes 2097152 | tf_op jit(solution)/shard_map/depth_in/all_to_all | solution.py:25
  153.2 14.5 %all-to-all-done.6 = bf16[4,1024,128]{2,1,0:T(8,128)(2,1)S(1)} async-done(((bf16[4,1024,128]{2,1,0:T(8,128)(2,1)}), bf16[4,1024,128]{2,1,0:T(8,128)(2,1)S(1)}, u32[]{:S(2)}, u32[]{:S(2)}) %all-to-all-start.6) | async-done | bytes 1048608 | tf_op jit(solution)/shard_map/depth_in/all_to_all | solution.py:25
  168.8 3.0 %fusion.11 = f32[8,96,128]{2,1,0:T(8,128)} fusion(bf16[8,288,1024]{2,1,0:T(8,128)(2,1)} %bitcast.203, f32[1024,128]{1,0:T(8,128)} %copy-done.3, f32[1024]{0:T(1024)S(1)} %bitcast.200, f32[128]{0:T(128)S(1)} %add_rsqrt_fusion.1), kind=kOutput, calls=%fused_computation.16 | convolution fusion | flops 201719808 | bytes 2494976 | tf_op jit(solution)/shard_map/depth_ff/zhd,dr->zhr/dot_general | solution.py:183
  171.9 3.8 %fusion.22 = bf16[1024,128]{1,0:T(8,128)(2,1)S(1)} fusion(bf16[8,288,1024]{2,1,0:T(8,128)(2,1)} %bitcast.204, f32[1024,128]{1,0:T(8,128)S(1)} %copy-done.4, f32[8,96,128]{2,1,0:T(8,128)} %fusion.11, f32[1024]{0:T(1024)S(1)} %bitcast.201, f32[128]{0:T(128)S(1)} %add_rsqrt_fusion.1), kind=kOutput, calls=%fused_computation.24 | convolution fusion | flops 404029440 | bytes 4854272 | tf_op jit(solution)/shard_map/depth_ff/zhn,zhr->nr/dot_general | solution.py:190
  176.4 3.4 %all-to-all-start.7 = ((bf16[4,8,32,128]{3,2,1,0:T(8,128)(2,1)}), bf16[4,8,32,128]{3,2,1,0:T(8,128)(2,1)S(1)}, u32[]{:S(2)}, u32[]{:S(2)}) async-start(bf16[4,8,32,128]{3,2,1,0:T(8,128)(2,1)} %bitcast.164), calls=%async_computation.7 | async-start | bytes 524288 | tf_op jit(solution)/shard_map/depth_ff/all_to_all | solution.py:25
  180.3 5.0 %all-to-all-done.7 = bf16[4,8,32,128]{3,2,1,0:T(8,128)(2,1)S(1)} async-done(((bf16[4,8,32,128]{3,2,1,0:T(8,128)(2,1)}), bf16[4,8,32,128]{3,2,1,0:T(8,128)(2,1)S(1)}, u32[]{:S(2)}, u32[]{:S(2)}) %all-to-all-start.7) | async-done | bytes 262176 | tf_op jit(solution)/shard_map/depth_ff/all_to_all | solution.py:25
  185.3 14.3 %all_to_all.46 = bf16[16,32,128]{2,1,0:T(8,128)(2,1)S(1)} all-to-all(bf16[16,32,128]{2,1,0:T(8,128)(2,1)S(1)} %pad_maximum_fusion.6), channel_id=1, replica_groups=mesh['cb'=4,'z'=8,'y'=4,'core'=2] {'z','core'}, dimensions={0} | all-to-all | bytes 262144 | tf_op jit(solution)/shard_map/place_outputs/all_to_all | solution.py:25
  (145 shorter events, 40.7 us)
Async XLA Ops:
  7.2 95.2 %copy-start = (bf16[4,64,4096]{2,1,0:T(8,128)(2,1)S(1)}, bf16[4,64,4096]{2,1,0:T(8,128)(2,1)}, u32[]{:S(2)}) copy-start(bf16[4,64,4096]{2,1,0:T(8,128)(2,1)} %param.18) | copy-start | bytes 6291460
  7.2 111.4 %all-gather.7.cloned.1.call-start = ((), (), s32[]{:S(2)}) async-start(), calls=%async_computation.10 | async-start | bytes 4718592 | tf_op jit(solution)/shard_map/pack_weights/all_gather | solution.py:68
  8.3 6.8 %copy-start.9 = (bf16[256,64]{0,1:T(8,128)(2,1)S(1)}, bf16[256,64]{0,1:T(8,128)(2,1)}, u32[]{:S(2)}) copy-start(bf16[256,64]{0,1:T(8,128)(2,1)} %param.13) | copy-start | bytes 98308
  8.3 6.8 %copy-start.12 = (bf16[64]{0:T(256)(128)(2,1)S(1)}, bf16[64]{0:T(256)(128)(2,1)}, u32[]{:S(2)}) copy-start(bf16[64]{0:T(256)(128)(2,1)} %param.14) | copy-start | bytes 388
  9.3 4.8 %collective-permute-start.1 = (bf16[96,1024]{1,0:T(8,128)(2,1)S(1)}, bf16[96,1024]{1,0:T(8,128)(2,1)S(1)}, u32[]{:S(2)}, u32[]{:S(2)}) collective-permute-start(bf16[96,1024]{1,0:T(8,128)(2,1)S(1)} %pad_maximum_fusion.3), channel_id=1, source_target_pairs={{0,1},{1,0},{2,3},{3,2},{4,5},{5,4},{6,7},{7,6},{8,9},{9,8},{10,11... | collective-permute-start | bytes 589832 | tf_op jit(solution)/shard_map/pack_weights/ppermute | solution.py:35
  35.1 19.5 %all-to-all-start.1 = ((bf16[4,8,72,256]{3,2,1,0:T(8,128)(2,1)}), bf16[4,8,72,256]{3,2,1,0:T(8,128)(2,1)S(1)}, u32[]{:S(2)}, u32[]{:S(2)}) async-start(bf16[4,8,72,256]{3,2,1,0:T(8,128)(2,1)} %broadcast_in_dim.116), calls=%async_computation.1 | async-start | bytes 2359296 | tf_op jit(solution)/shard_map/gather_hidden/all_to_all | solution.py:25
  39.4 18.6 %copy-start.5 = (bf16[2,44,1024]{2,0,1:T(2,128)(2,1)S(1)}, bf16[2,44,1024]{2,0,1:T(2,128)(2,1)}, u32[]{:S(2)}) copy-start(bf16[2,44,1024]{2,0,1:T(2,128)(2,1)} %param.25) | copy-start | bytes 540676
  39.4 129.5 %all-gather.5.cloned.1.call-start = ((), (), s32[]{:S(2)}) async-start(), calls=%async_computation.9 | async-start | bytes 5308416 | tf_op jit(solution)/shard_map/pack_weights/all_gather | solution.py:76
  54.6 4.4 %copy-start.6 = (bf16[1,2,1024,44]{2,1,3,0:T(2,128)(2,1)S(1)}, bf16[1,2,1024,44]{2,1,3,0:T(2,128)(2,1)}, u32[]{:S(2)}) copy-start(bf16[1,2,1024,44]{2,1,3,0:T(2,128)(2,1)} %get-tuple-element.19) | copy-start | bytes 540676
  54.6 4.4 %copy-start.7 = (bf16[1,2,1024,44]{2,1,3,0:T(2,128)(2,1)S(1)}, bf16[1,2,1024,44]{2,1,3,0:T(2,128)(2,1)}, u32[]{:S(2)}) copy-start(bf16[1,2,1024,44]{2,1,3,0:T(2,128)(2,1)} %get-tuple-element.20) | copy-start | bytes 540676
  55.7 20.4 %collective-permute-start.2 = (bf16[4,8,72,256]{3,2,0,1:T(8,128)(2,1)}, bf16[4,8,72,256]{3,2,0,1:T(8,128)(2,1)}, u32[]{:S(2)}, u32[]{:S(2)}) collective-permute-start(bf16[4,8,72,256]{3,2,0,1:T(8,128)(2,1)} %copy.105), channel_id=1, source_target_pairs={{0,1},{1,0},{2,3},{3,2},{4,5},{5,4},{6,7},{7,6},{8,9},{9,8},{10,11... | collective-permute-start | bytes 3538952 | tf_op jit(solution)/shard_map/gather_hidden/ppermute | solution.py:35
  59.9 3.7 %collective-permute-start = (bf16[132,1024]{1,0:T(8,128)(2,1)}, bf16[132,1024]{1,0:T(8,128)(2,1)}, u32[]{:S(2)}, u32[]{:S(2)}) collective-permute-start(bf16[132,1024]{1,0:T(8,128)(2,1)} %pad_maximum_fusion.2), channel_id=1, source_target_pairs={{0,1},{1,0},{2,3},{3,2},{4,5},{5,4},{6,7},{7,6},{8,9},{9,8},{10,11... | collective-permute-start | bytes 811016 | tf_op jit(solution)/shard_map/pack_weights/ppermute | solution.py:35
  79.8 6.4 %copy-start.11 = (s32[1024,2]{0,1:T(2,128)S(1)}, s32[1024,2]{0,1:T(2,128)}, u32[]{:S(2)}) copy-start(s32[1024,2]{0,1:T(2,128)} %param.20) | copy-start | bytes 24580
  79.8 6.8 %copy-start.14 = (s32[4]{0:T(128)S(1)}, s32[4]{0:T(128)}, u32[]{:S(2)}) copy-start(s32[4]{0:T(128)} %param.19) | copy-start | bytes 52
  81.5 16.9 %all-to-all-start.2 = ((bf16[64,4,256]{2,1,0:T(4,128)(2,1)}), bf16[64,4,256]{2,1,0:T(4,128)(2,1)S(1)}, u32[]{:S(2)}, u32[]{:S(2)}) async-start(bf16[64,4,256]{2,1,0:T(4,128)(2,1)} %pad_maximum_fusion.5), calls=%async_computation.2 | async-start | bytes 262144 | tf_op jit(solution)/shard_map/qkv/all_to_all | solution.py:25
  102.0 8.4 %copy-start.13 = (s32[2]{0:T(128)S(1)}, s32[2]{0:T(128)}, u32[]{:S(2)}) copy-start(s32[2]{0:T(128)} %iota_multiply_fusion) | copy-start | bytes 28
  104.4 14.1 %all-to-all-start.3 = ((bf16[32,4,640]{2,1,0:T(4,128)(2,1)}), bf16[32,4,640]{2,1,0:T(4,128)(2,1)S(1)}, u32[]{:S(2)}, u32[]{:S(2)}) async-start(bf16[32,4,640]{2,1,0:T(4,128)(2,1)} %pad_maximum_fusion.4), calls=%async_computation.3 | async-start | bytes 327680 | tf_op jit(solution)/shard_map/project/all_to_all | solution.py:25
  123.0 10.2 %all-to-all-start.4 = ((bf16[8,128,128]{2,1,0:T(8,128)(2,1)}), bf16[8,128,128]{2,1,0:T(8,128)(2,1)S(1)}, u32[]{:S(2)}, u32[]{:S(2)}) async-start(bf16[8,128,128]{2,1,0:T(8,128)(2,1)} %bitcast.176), calls=%async_computation.4 | async-start | bytes 524288 | tf_op jit(solution)/shard_map/project/all_to_all | solution.py:25
  128.6 9.4 %collective-permute-start.4 = (bf16[2,8,16,128]{3,2,1,0:T(8,128)(2,1)S(1)}, bf16[2,8,16,128]{3,2,1,0:T(8,128)(2,1)S(1)}, u32[]{:S(2)}, u32[]{:S(2)}) collective-permute-start(bf16[2,8,16,128]{3,2,1,0:T(8,128)(2,1)S(1)} %fusion.35), channel_id=1, source_target_pairs={{0,64},{64,128},{128,192},{192,0},{2,66},{66,130},{130,194},{194,2... | collective-permute-start | bytes 196616 | tf_op jit(solution)/shard_map/embed/ppermute | solution.py:162
  134.7 8.1 %all-to-all-start.5 = ((bf16[4,128,128]{2,1,0:T(8,128)(2,1)}), bf16[4,128,128]{2,1,0:T(8,128)(2,1)S(1)}, u32[]{:S(2)}, u32[]{:S(2)}) async-start(bf16[4,128,128]{2,1,0:T(8,128)(2,1)} %broadcast_in_dim.120), calls=%async_computation.5 | async-start | bytes 262144 | tf_op jit(solution)/shard_map/project/all_to_all | solution.py:25
  142.8 3.1 %collective-permute-start.3 = (bf16[4,128,128]{2,1,0:T(8,128)(2,1)S(1)}, bf16[4,128,128]{2,1,0:T(8,128)(2,1)S(1)}, u32[]{:S(2)}, u32[]{:S(2)}) collective-permute-start(bf16[4,128,128]{2,1,0:T(8,128)(2,1)S(1)} %all-to-all-done.5), channel_id=1, source_target_pairs={{0,1},{1,0},{2,3},{3,2},{4,5},{5,4},{6,7},{7,6},{8,9},{9,8},{10,11... | collective-permute-start | bytes 393224 | tf_op jit(solution)/shard_map/project/ppermute | solution.py:35
  148.2 4.9 %copy-start.10 = (bf16[2,1024]{1,0:T(2,128)(2,1)S(1)}, bf16[2,1024]{1,0:T(2,128)(2,1)}, u32[]{:S(2)}) copy-start(bf16[2,1024]{1,0:T(2,128)(2,1)} %param.23) | copy-start | bytes 12292
  149.4 18.3 %all-to-all-start.6 = ((bf16[4,1024,128]{2,1,0:T(8,128)(2,1)}), bf16[4,1024,128]{2,1,0:T(8,128)(2,1)S(1)}, u32[]{:S(2)}, u32[]{:S(2)}) async-start(bf16[4,1024,128]{2,1,0:T(8,128)(2,1)} %broadcast_in_dim.127), calls=%async_computation.6 | async-start | bytes 2097152 | tf_op jit(solution)/shard_map/depth_in/all_to_all | solution.py:25
  176.4 8.9 %all-to-all-start.7 = ((bf16[4,8,32,128]{3,2,1,0:T(8,128)(2,1)}), bf16[4,8,32,128]{3,2,1,0:T(8,128)(2,1)S(1)}, u32[]{:S(2)}, u32[]{:S(2)}) async-start(bf16[4,8,32,128]{3,2,1,0:T(8,128)(2,1)} %bitcast.164), calls=%async_computation.7 | async-start | bytes 524288 | tf_op jit(solution)/shard_map/depth_ff/all_to_all | solution.py:25
  (5 other events, 11.4 us)
Sparse Core Ops, SparseCore 0:
  15.2 57.0 all-gather.6
  76.2 58.6 all-gather.4

commit v2 on v1

v2 whole, which is shorter than its diff:
```python
import math

import jax
import jax.numpy as jnp
from jax import lax
from jax.experimental import pallas as pl
from jax.experimental.pallas import tpu as pltpu
from jax.sharding import Mesh, PartitionSpec as P

D = 4096
HEADS = 32
HEAD_DIM = 128
DD = 1024
CARD = 2048
CACHE = 64
X, Z, Y, C = 4, 8, 4, 2
HID = 44
HID_PAD = 48

eps = 1e-05
BF = jnp.bfloat16
F32 = jnp.float32
TP = ("z", "y", "core")


def exchange(value, axis):
    return lax.all_to_all(value, axis, split_axis=0, concat_axis=0, tiled=True)


def spread(value, axis):
    count = lax.axis_size(axis)
    copies = jnp.broadcast_to(value[None], (count,) + value.shape)
    return exchange(copies, axis)


def from_each(value, axis):
    count = lax.axis_size(axis)
    return [value] + [
        lax.ppermute(value, axis, [(i, (i + step) % count) for i in range(count)])
        for step in range(1, count)
    ]


def ring_halves(low, high, axis):
    up = [(i, (i + 1) % 4) for i in range(4)]
    down = [(i, (i + 3) % 4) for i in range(4)]
    low_behind = lax.ppermute(low, axis, up)
    high_ahead = lax.ppermute(high, axis, down)
    high_behind = lax.ppermute(high, axis, up)
    low_ahead = lax.ppermute(low, axis, down)
    low_across = lax.ppermute(low_behind, axis, up)
    high_across = lax.ppermute(high_ahead, axis, down)
    return (low_behind, high_behind), (low_ahead, high_ahead), (low_across, high_across)


def swap(value):
    return lax.ppermute(value, "core", [(0, 1), (1, 0)])


def pick(value, index):
    return lax.dynamic_index_in_dim(value, index, 0, keepdims=False)


def dot_nt(a, b):
    return lax.dot_general(a, b, (((1,), (1,)), ((), ())), preferred_element_type=F32)


def in_vmem(kernel, out_shape, flops, args):
    return pl.pallas_call(
        kernel,
        in_specs=[pl.BlockSpec(memory_space=pltpu.VMEM)] * len(args),
        out_specs=pl.BlockSpec(memory_space=pltpu.VMEM),
        out_shape=jax.ShapeDtypeStruct(out_shape, BF),
        compiler_params=pltpu.CompilerParams(vmem_limit_bytes=24 * 1024 * 1024),
        cost_estimate=pl.CostEstimate(
            flops=flops, bytes_accessed=sum(a.size * 2 for a in args), transcendentals=0
        ),
    )(*args)


def prepare_kernel(hid_ref, emb_ref, token_ref, hid_out, emb_out):
    row = lax.broadcasted_iota(jnp.int32, (256, 256), 0)
    col = lax.broadcasted_iota(jnp.int32, (256, 256), 1)
    within = col % 128
    chosen = (row == (within // 4) * 8 + within % 4 + 4 * (col // 128)).astype(BF)
    split = jnp.dot(hid_ref[...], chosen, preferred_element_type=F32).astype(BF)
    hid_out[0] = split[:, :128]
    hid_out[1] = split[:, 128:]
    low_codes = lax.broadcasted_iota(jnp.int32, (128, 1024), 0)
    for core in range(C):
        index = 1 - core
        token = token_ref[index : index + 1]
        low = (low_codes == token % 128).astype(BF)
        high = token // 128
        table = jnp.concatenate(
            [emb_ref[index, :, h * 128 : (h + 1) * 128] for h in range(16)], axis=0
        )
        found = jnp.dot(table, low, preferred_element_type=F32)
        total = jnp.zeros((16, 1024), F32)
        for h in range(16):
            total += jnp.where(high == h, found[h * 16 : (h + 1) * 16], 0.0)
        for z in range(Z):
            emb_out[z, core] = jnp.concatenate(
                [total[:, x * 256 + z * 32 : x * 256 + z * 32 + 32] for x in range(X)], axis=1
            ).astype(BF)


def prepare(hid_t, emb_t, token):
    return pl.pallas_call(
        prepare_kernel,
        in_specs=[pl.BlockSpec(memory_space=pltpu.VMEM)] * 3,
        out_specs=[pl.BlockSpec(memory_space=pltpu.VMEM)] * 2,
        out_shape=[
            jax.ShapeDtypeStruct((C, 64, 128), BF),
            jax.ShapeDtypeStruct((Z, C, 16, 128), BF),
        ],
        compiler_params=pltpu.CompilerParams(vmem_limit_bytes=24 * 1024 * 1024),
    )(hid_t, emb_t, token)


def project_kernel(moved_ref, w_ref, out_ref):
    acc = jnp.zeros((128, DD), F32)
    for i in range(4):
        acc += jnp.dot(
            moved_ref[:, i * 128 : (i + 1) * 128],
            w_ref[2 * i : 2 * i + 2, 128:].reshape(128, DD),
            preferred_element_type=F32,
        )
    for block in range(8):
        low = acc[:, block * 64 : (block + 1) * 64]
        high = acc[:, 512 + block * 64 : 512 + (block + 1) * 64]
        out_ref[block] = jnp.concatenate([low, high], axis=1).astype(BF)


def depth_in_kernel(own_ref, oth_ref, w_ref, emb_ref, out_ref):
    acc = emb_ref[...].astype(F32)
    for i in range(X):
        w = w_ref[2 * i : 2 * i + 2, :128]
        acc += jnp.dot(own_ref[i], w[:, :64].reshape(128, DD), preferred_element_type=F32)
        acc += jnp.dot(oth_ref[i], w[:, 64:].reshape(128, DD), preferred_element_type=F32)
    out_ref[...] = acc.astype(BF)


def depth_ff_kernel(a_ref, b_ref, c_ref, d_ref, gain_ref, w_ref, out_ref):
    x = a_ref[...].astype(F32) + b_ref[...].astype(F32)
    x = x + c_ref[...].astype(F32) + d_ref[...].astype(F32)
    mean = jnp.sum(x * x, axis=1, keepdims=True) / DD
    xn = (x * lax.rsqrt(mean + eps) * gain_ref[...]).astype(BF)
    acc = x * (1.0 / Y)
    wide = 2 * HID_PAD
    for i in range(4):
        w = w_ref.at[2 * i : 2 * i + 2]
        gate = dot_nt(xn, w[:, :wide].reshape(2 * wide, DD))
        upper = dot_nt(xn, w[:, wide : 2 * wide].reshape(2 * wide, DD))
        act = (jax.nn.silu(gate) * upper).astype(BF)
        acc += jnp.dot(
            act, w[:, 2 * wide :].reshape(2 * wide, DD), preferred_element_type=F32
        )
    for block in range(Z):
        turned = acc[:, block * 128 : (block + 1) * 128].T
        out_ref[block] = turned.reshape(Y, 32, 128).astype(BF)


def per_device(
    hidden_in,
    norm_gain,
    w_qkv,
    w_out,
    cache_keys,
    cache_values,
    lengths,
    tokens,
    w_in,
    embed,
    depth_gain,
    w_gate_up,
    w_down,
):
    xi, zi, yi, ci = (lax.axis_index(a) for a in ("cb", "z", "y", "core"))
    other = 1 - ci

    with jax.named_scope("gather_hidden"):
        hid_split, emb_sent = prepare(hidden_in.T, embed.transpose(0, 2, 1), tokens.T)
        gain_row = jnp.pad(norm_gain[None, :], ((0, 7), (0, 64)))
        copies = jnp.concatenate(
            [
                jnp.broadcast_to(hid_split[None], (Z, C, 64, 128)),
                jnp.broadcast_to(gain_row, (Z, C, 8, 128)),
                emb_sent,
            ],
            axis=2,
        )
        column = exchange(copies.reshape(16, 88, 128), ("z", "core")).reshape(Z, C, 88, 128)
        emb_here = column[:, :, 72:]
        started = swap(hid_split[0, :16])
        w_in, w_out, w_gate_up, w_down, w_qkv, started = lax.optimization_barrier(
            (w_in, w_out, w_gate_up, w_down, w_qkv, started)
        )

    with jax.named_scope("pack_weights"):
        recv_a = swap(pick(w_in, other))
        wo = lax.dynamic_slice_in_dim(w_out, xi * DD, DD, 1)
        first_in = jnp.concatenate([pick(w_in, ci), recv_a, wo], axis=0)
        gu_t = w_gate_up.transpose(0, 3, 1, 2)
        gap = ((0, HID_PAD - HID), (0, 0))

        def stacked(step):
            gu = pick(gu_t, step)
            parts = (gu[:, 0], gu[:, 1], pick(w_down, step))
            return [jnp.pad(part, gap) for part in parts]

        recv_b = swap(jnp.concatenate(stacked(other), axis=0))
        second_in = []
        for index, part in enumerate(stacked(ci)):
            second_in += [part, recv_b[index * HID_PAD : (index + 1) * HID_PAD]]
        second_in = jnp.concatenate(second_in, axis=0)
        first = lax.all_gather(first_in, "z")
        second = lax.all_gather(second_in, "z")

    with jax.named_scope("norm"):
        w_own = w_qkv.transpose(0, 2, 1).reshape(192, D)
        w_oth = swap(w_own)
        halves = (column[:4, :, :72], column[4:, :, :72])
        pieces = [(halves, 0)] + list(zip(ring_halves(*halves, "y"), (3, 1, 2)))
        blocks = [
            (part, index * 4, lax.rem(yi + step, Y))
            for parts, step in pieces
            for index, part in enumerate(parts)
        ]
        sum_sq = sum(
            jnp.sum(jnp.square(part[:, :, :64].astype(F32)), axis=(0, 1, 2))
            for part, _, _ in blocks
        )
        inv = lax.rsqrt(sum_sq / D + eps)
        normed = jnp.zeros((Z, Y, C, 64, 128), BF)
        for part, at_z, at_y in blocks:
            gain = part[:, :, 64, :64].astype(F32)[..., None]
            block = (part[:, :, :64].astype(F32) * inv * gain).astype(BF)
            normed = lax.dynamic_update_slice(normed, block[:, None], (at_z, at_y, 0, 0, 0))
        normed = normed.reshape(D, 128)

    with jax.named_scope("qkv"):
        q_own = jnp.einsum("dr,nd->rn", normed, w_own, preferred_element_type=F32).astype(BF)
        q_oth = jnp.einsum("dr,nd->rn", normed, w_oth, preferred_element_type=F32).astype(BF)
        q_low = jnp.where(ci == 0, q_own, q_oth).reshape(128, 3, 64)
        q_high = jnp.where(ci == 0, q_oth, q_own).reshape(128, 3, 64)
        hid_cols = pick(column, zi)[:, :64]
        qkv = jnp.concatenate([q_low, q_high], axis=2).reshape(128, 384)
        sent = jnp.concatenate([qkv, hid_cols.reshape(128, 128).T], axis=1)
        got = exchange(sent.reshape(32, 4, 512), ("z", "y"))
        got = got.reshape(HEADS, 4, 4, HEAD_DIM).transpose(1, 2, 0, 3)

    with jax.named_scope("embed"):
        moved_emb = lax.ppermute(
            emb_here, ("cb", "core"), [(2 * x, 2 * ((x + 1) % X)) for x in range(X)]
        )
        emb = jnp.where(ci == 0, moved_emb, emb_here).reshape(256, 128)
        source = lax.broadcasted_iota(jnp.int32, (256, DD), 0)
        target = lax.broadcasted_iota(jnp.int32, (256, DD), 1)
        place = (target == (source // 32) * 128 + yi * 32 + source % 32).astype(BF)
        emb = jnp.dot(emb.T, place, preferred_element_type=F32).astype(BF)

    with jax.named_scope("attend"):
        got, first = lax.optimization_barrier((got, first))
        query_h, key_new, value_new = got[:, 0], got[:, 1], got[:, 2]
        hid_rows = got[:, 3]
        scale = 1.0 / math.sqrt(HEAD_DIM)
        keys_h = cache_keys.reshape(4, CACHE, HEADS, HEAD_DIM)
        values_h = cache_values.reshape(4, CACHE, HEADS, HEAD_DIM)
        scores = jnp.einsum("rhe,rphe->rhp", query_h, keys_h, preferred_element_type=F32) * scale
        live = lax.broadcasted_iota(jnp.int32, (1, 1, CACHE), 2) < lengths[:, None, None]
        scores = jnp.where(live, scores, -1e30)
        fresh = jnp.sum(query_h.astype(F32) * key_new.astype(F32), axis=-1) * scale
        top = jnp.maximum(jnp.max(scores, axis=-1), fresh)
        weights = jnp.exp(scores - top[..., None])
        weight_new = jnp.exp(fresh - top)
        total = jnp.sum(weights, axis=-1) + weight_new
        probs = (weights / total[..., None]).astype(BF)
        prob_new = (weight_new / total).astype(BF)
        mixed = jnp.einsum("rhp,rphe->rhe", probs, values_h, preferred_element_type=F32)
        mixed = mixed + prob_new.astype(F32)[..., None] * value_new.astype(F32)
        attended = mixed.astype(BF)

    with jax.named_scope("project"):
        att = attended.reshape(4, Z, Y, C, 64).transpose(2, 3, 0, 1, 4).reshape(1, 8, 4, 512)
        att = jnp.broadcast_to(att, (X, 8, 4, 512))
        res = hid_rows.reshape(4, X, 2, Y, C, 64).transpose(1, 3, 4, 0, 2, 5)
        res = res.reshape(X, 8, 4, 128)
        moved = exchange(
            jnp.concatenate([att, res], axis=-1).reshape(32, 4, 640), ("cb", "y", "core")
        ).reshape(128, 640)
        part = in_vmem(project_kernel, (8, 128, 128), 2 * 128 * 512 * DD, (moved[:, :512], first))
        part = exchange(part, ("y", "core"))
        temporal = jnp.sum(part.astype(F32), axis=0) + moved[:, 512:].astype(F32)
        temporal = temporal.astype(BF)
        around = from_each(temporal, "cb")
        frame = jnp.zeros((X, 128, 128), BF)
        for step, piece in enumerate(around):
            at = lax.rem(xi - step + X, X)
            frame = lax.dynamic_update_slice(frame, piece[None], (at, 0, 0))
        frame_oth = swap(frame)

    with jax.named_scope("depth"):
        x_part = in_vmem(
            depth_in_kernel, (128, DD), 2 * 128 * 1024 * DD, (frame, frame_oth, first, emb)
        )
        gain_d = lax.dynamic_slice_in_dim(depth_gain, ci, 1, 0).astype(F32)
        out = in_vmem(
            depth_ff_kernel,
            (Z, Y, 32, 128),
            6 * 128 * 768 * DD,
            (*from_each(x_part, "y"), gain_d, second),
        )
        out = exchange(out.reshape(64, 16, 128), TP).reshape(Z, Y, C, 16, 128)
        out = jnp.sum(out.astype(F32), axis=1).astype(BF)

    with jax.named_scope("place_outputs"):
        depth_out = out.reshape(Z, C, 16, X, 32).transpose(1, 3, 0, 4, 2)
        depth_out = depth_out.reshape(C, 1024, 16)
        rows = lax.dynamic_slice_in_dim(frame, xi * 32, 32, 1)
        rows = rows.reshape(X, 2, 16, 2, 64).transpose(0, 3, 2, 1, 4).reshape(Z, 16, 128)
        rows = exchange(rows, "z")
        temporal_out = rows.reshape(Z, 16, 2, 64).transpose(0, 2, 1, 3).reshape(256, 64)
    return (temporal_out, depth_out)


def solution(mesh):
    fine = Mesh(mesh.devices.reshape(X, Z, Y, C), ("cb", "z", "y", "core"))
    every = ("cb",) + TP
    in_specs = (
        P("cb", TP),
        P(TP),
        P(None, None, TP),
        P(TP, None),
        P(every, None, None),
        P(every, None, None),
        P(every),
        P(None, "cb"),
        P("cb", TP, None),
        P("cb", None, TP),
        P("cb", None),
        P("cb", None, None, TP),
        P("cb", TP, None),
    )
    out_specs = (P("cb", TP), P("cb", None, TP))
    return jax.shard_map(
        per_device, mesh=fine, in_specs=in_specs, out_specs=out_specs, check_vma=False
    )
```

time: 210 us -> 171 us (0.81)
  local copies, waits for them, and re-layouts: 38.5 us -> 14.1 us
  blocking collectives: 33.1 us -> 15.5 us
  starting transfers between devices: 37.7 us -> 48.8 us
  matrix products: 14 us -> 6.44 us
  Pallas kernels: 0 us -> 5.32 us
  other arithmetic: 10.4 us -> 6.16 us
    all_to_all x7 -> x5, waiting for transfers between devices: 59.5 us -> 39 us  [exchange(): return lax.all_to_all(value, axis, split_axis=0, concat_axis=0, tiled=True)]
    all_to_all x2 -> x1, blocking collectives: 33.1 us -> 15.5 us  [exchange(): return lax.all_to_all(value, axis, split_axis=0, concat_axis=0, tiled=True)]
    ppermute x1 -> x13, waiting for transfers between devices: 0.01 us -> 16.9 us  [the longest x6 8.52 us: from_each(): lax.ppermute(value, axis, [(i, (i + step) % count) for i in range(count)])]
    ppermute x1 -> x13, starting transfers between devices: 0.85 us -> 15.4 us  [the longest x6 7.41 us: from_each(): lax.ppermute(value, axis, [(i, (i + step) % count) for i in range(count)])]
    concatenate x2, local copies, waits for them, and re-layouts: 11.1 us -> 0.09 us  [the longest x1 0.08 us: per_device(): sent = jnp.concatenate([qkv, hid_cols.reshape(128, 128).T], axis=1)]
    slice x5 -> x4, local copies, waits for them, and re-layouts: 7.39 us -> 0.05 us  [the longest x1 0.02 us: per_device(): halves = (column[:4, :, :72], column[4:, :, :72])]
    dot_general x5 -> x3, matrix products: 9.99 us -> 3.03 us  [the longest x1 1.98 us: per_device(): jnp.einsum('dr,nd->rn', normed, w_oth, preferred_element_type=F32)]
    pallas_call x0 -> x4, Pallas kernels: none -> 5.32 us  [the longest x3 4.75 us: in_vmem(): pl.pallas_call(kernel, in_specs=[pl.BlockSpec(memory_space=pltpu.VMEM)] *...]
  transfers between devices with their start and end apart: 14 -> 24, of which waited for: 8 -> 15; matrix products, arithmetic and copies ran while one was open for 23% -> 10% of each run, Pallas kernels for 0% -> 3%
where the time goes in v2:
time: 171 us; the launch traced here: 170 us
  waiting for transfers between devices  59.1 us (35%)
  starting transfers between devices  48.8 us (29%)
  blocking collectives  15.5 us (9%)
  between operations  14.7 us (9%)
  local copies, waits for them, and re-layouts  14.1 us (8%)
  matrix products  6.44 us (4%)
  other arithmetic  6.16 us (4%)
  Pallas kernels  5.32 us (3%)
    all_to_all x5, waiting for transfers between devices, exchange(): return lax.all_to_all(value, axis, split_axis=0, concat_axis=0, tiled=True)  39 us
    all_to_all x5, starting transfers between devices, exchange(): return lax.all_to_all(value, axis, split_axis=0, concat_axis=0, tiled=True)  27.2 us
    all_to_all x1, blocking collectives, exchange(): return lax.all_to_all(value, axis, split_axis=0, concat_axis=0, tiled=True)  15.5 us
    ppermute x6, waiting for transfers between devices, from_each(): lax.ppermute(value, axis, [(i, (i + step) % count) for i in range(count)])  8.52 us
    ppermute x6, starting transfers between devices, from_each(): lax.ppermute(value, axis, [(i, (i + step) % count) for i in range(count)])  7.41 us
    unnamed x32, local copies, waits for them, and re-layouts  7.33 us
    ppermute x4, starting transfers between devices, swap(): return lax.ppermute(value, 'core', [(0, 1), (1, 0)])  6.08 us
    pallas_call x3, Pallas kernels, in_vmem(): pl.pallas_call(kernel, in_specs=[pl.BlockSpec(memory_space=pltpu.VMEM)] *...  4.75 us
  transfers between devices with their start and end apart: 24, of which 15 were waited for; matrix products, arithmetic and copies ran while one was open for 10% of the time, Pallas kernels for 3%

profile of v2, /device:TPU:1, one launch (start us, length us, event | category | flops | bytes accessed | tf_op | source)
XLA Modules:
  0.0 170.1 jit_solution(14414446992067274172)
XLA Ops:
  8.4 3.3 %collective-permute-start.7 = (bf16[64,1024]{1,0:T(8,128)(2,1)S(1)}, bf16[64,1024]{1,0:T(8,128)(2,1)S(1)}, u32[]{:S(2)}, u32[]{:S(2)}) collective-permute-start(bf16[64,1024]{1,0:T(8,128)(2,1)S(1)} %get-tuple-element.37), channel_id=1, source_target_pairs={{0,1},{1,0},{2,3},{3,2},{4,5},{5,4},{6,7},{7,6},{8,9},{9,8},{10,11... | collective-permute-start | bytes 393224 | tf_op jit(solution)/shard_map/pack_weights/ppermute | solution.py:57
  17.1 7.1 %all-to-all-start = ((bf16[16,88,128]{2,1,0:T(8,128)(2,1)}), bf16[16,88,128]{2,1,0:T(8,128)(2,1)S(1)}, u32[]{:S(2)}, u32[]{:S(2)}) async-start(bf16[16,88,128]{2,1,0:T(8,128)(2,1)} %bitcast.4), calls=%async_computation | async-start | bytes 720896 | tf_op jit(solution)/shard_map/gather_hidden/all_to_all | solution.py:27
  25.8 2.5 %collective-permute-done.16 = bf16[144,1024]{1,0:T(8,128)(2,1)S(1)} collective-permute-done((bf16[144,1024]{1,0:T(8,128)(2,1)}, bf16[144,1024]{1,0:T(8,128)(2,1)S(1)}, u32[]{:S(2)}, u32[]{:S(2)}) %collective-permute-start.16) | collective-permute-done | bytes 294944 | tf_op jit(solution)/shard_map/pack_weights/ppermute | solution.py:57
  29.3 11.8 %all-to-all-done = bf16[16,88,128]{2,1,0:T(8,128)(2,1)S(1)} async-done(((bf16[16,88,128]{2,1,0:T(8,128)(2,1)}), bf16[16,88,128]{2,1,0:T(8,128)(2,1)S(1)}, u32[]{:S(2)}, u32[]{:S(2)}) %all-to-all-start) | async-done | bytes 360480 | tf_op jit(solution)/shard_map/gather_hidden/all_to_all | solution.py:27
  45.8 2.1 %collective-permute-done = bf16[4,2,72,128]{3,2,1,0:T(8,128)(2,1)S(1)} collective-permute-done((bf16[4,2,72,128]{3,2,1,0:T(8,128)(2,1)S(1)}, bf16[4,2,72,128]{3,2,1,0:T(8,128)(2,1)S(1)}, u32[]{:S(2)}, u32[]{:S(2)}) %collective-permute-start) | collective-permute-done | bytes 147488 | tf_op jit(solution)/shard_map/norm/ppermute | solution.py:47
  48.0 3.4 %collective-permute-done.3 = bf16[4,2,72,128]{3,2,1,0:T(8,128)(2,1)S(1)} collective-permute-done((bf16[4,2,72,128]{3,2,1,0:T(8,128)(2,1)S(1)}, bf16[4,2,72,128]{3,2,1,0:T(8,128)(2,1)S(1)}, u32[]{:S(2)}, u32[]{:S(2)}) %collective-permute-start.3) | collective-permute-done | bytes 147488 | tf_op jit(solution)/shard_map/norm/ppermute | solution.py:48
  51.5 2.6 %collective-permute-start.5 = (bf16[4,2,72,128]{3,2,1,0:T(8,128)(2,1)S(1)}, bf16[4,2,72,128]{3,2,1,0:T(8,128)(2,1)S(1)}, u32[]{:S(2)}, u32[]{:S(2)}) collective-permute-start(bf16[4,2,72,128]{3,2,1,0:T(8,128)(2,1)S(1)} %collective-permute-done.3), channel_id=1, source_target_pairs={{0,6},{2,0},{4,2},{6,4},{1,7},{3,1},{5,3},{7,5},{8,14},{10,8},{12,... | collective-permute-start | bytes 442376 | tf_op jit(solution)/shard_map/norm/ppermute | solution.py:52
  54.5 2.9 %collective-permute-done.5 = bf16[4,2,72,128]{3,2,1,0:T(8,128)(2,1)S(1)} collective-permute-done((bf16[4,2,72,128]{3,2,1,0:T(8,128)(2,1)S(1)}, bf16[4,2,72,128]{3,2,1,0:T(8,128)(2,1)S(1)}, u32[]{:S(2)}, u32[]{:S(2)}) %collective-permute-start.5) | collective-permute-done | bytes 147488 | tf_op jit(solution)/shard_map/norm/ppermute | solution.py:52
  59.3 2.0 %convolution_convert_fusion.1 = bf16[128,192]{0,1:T(8,128)(2,1)S(1)} fusion(bf16[192,4096]{1,0:T(8,128)(2,1)} %collective-permute-done.6, bf16[4096,128]{1,0:T(8,128)(2,1)S(1)} %bitcast.176), kind=kOutput, calls=%fused_computation.7 | convolution fusion | flops 201351168 | bytes 2670592 | tf_op jit(solution)/shard_map/qkv/dr,nd->rn/dot_general | solution.py:244
  63.2 6.7 %all-to-all-start.1 = ((bf16[32,4,512]{2,1,0:T(4,128)(2,1)}), bf16[32,4,512]{2,1,0:T(4,128)(2,1)S(1)}, u32[]{:S(2)}, u32[]{:S(2)}) async-start(bf16[32,4,512]{2,1,0:T(4,128)(2,1)} %pad_maximum_fusion.4), calls=%async_computation.1 | async-start | bytes 262144 | tf_op jit(solution)/shard_map/qkv/all_to_all | solution.py:27
  70.0 9.1 %all-to-all-done.1 = bf16[32,4,512]{2,1,0:T(4,128)(2,1)S(1)} async-done(((bf16[32,4,512]{2,1,0:T(4,128)(2,1)}), bf16[32,4,512]{2,1,0:T(4,128)(2,1)S(1)}, u32[]{:S(2)}, u32[]{:S(2)}) %all-to-all-start.1) | async-done | bytes 131104 | tf_op jit(solution)/shard_map/qkv/all_to_all | solution.py:27
  79.6 2.8 %fusion.3 = f32[4,32,1,64]{3,2,1,0:T(1,128)S(1)} fusion(bf16[4,32,128,1]{2,1,0,3:T(8,128)(2,1)S(1)} %get-tuple-element.44, bf16[4,64,4096]{2,1,0:T(8,128)(2,1)} %param.17), kind=kOutput, calls=%fused_computation.3 | convolution fusion | flops 2097152 | bytes 2162688 | tf_op jit(solution)/shard_map/attend/rhe,rphe->rhp/dot_general | solution.py:270
  84.0 15.5 %all_to_all.30 = bf16[32,4,640]{2,1,0:T(4,128)(2,1)S(1)} all-to-all(bf16[32,4,640]{2,1,0:T(4,128)(2,1)S(1)} %pad_maximum_fusion.2), channel_id=1, replica_groups=mesh['cb'=4,'z'=8,'y'=4,'core'=2] {'cb','y','core'}, dimensions={0} | all-to-all | bytes 327680 | tf_op jit(solution)/shard_map/project/all_to_all | solution.py:27
  99.5 1.9 %copy-done.1 = bf16[1536,1024]{1,0:T(8,128)(2,1)S(1)} copy-done((bf16[1536,1024]{1,0:T(8,128)(2,1)S(1)}, bf16[1536,1024]{1,0:T(8,128)(2,1)}, u32[]{:S(2)}) %copy-start.1) | copy-done | bytes 3145752
  102.7 3.7 %all-to-all-start.3 = ((bf16[8,128,128]{2,1,0:T(8,128)(2,1)}), bf16[8,128,128]{2,1,0:T(8,128)(2,1)S(1)}, u32[]{:S(2)}, u32[]{:S(2)}) async-start(bf16[8,128,128]{2,1,0:T(8,128)(2,1)} %project.1), calls=%async_computation.3 | async-start | bytes 524288 | tf_op jit(solution)/shard_map/project/all_to_all | solution.py:27
  107.1 5.8 %all-to-all-done.3 = bf16[8,128,128]{2,1,0:T(8,128)(2,1)S(1)} async-done(((bf16[8,128,128]{2,1,0:T(8,128)(2,1)}), bf16[8,128,128]{2,1,0:T(8,128)(2,1)S(1)}, u32[]{:S(2)}, u32[]{:S(2)}) %all-to-all-start.3) | async-done | bytes 262176 | tf_op jit(solution)/shard_map/project/all_to_all | solution.py:27
  118.5 2.2 %collective-permute-start.11 = (bf16[4,128,128]{2,1,0:T(8,128)(2,1)S(1)}, bf16[4,128,128]{2,1,0:T(8,128)(2,1)S(1)}, u32[]{:S(2)}, u32[]{:S(2)}) collective-permute-start(bf16[4,128,128]{2,1,0:T(8,128)(2,1)S(1)} %bitcast_dynamic-update-slice_fusion.own_ref), channel_id=1, source_target_pairs={{0,1},{1,0},{2,3},{3,2},{4,5},{5,4},{6,7},{7,6},{8,9},{9,8},{10,11... | collective-permute-start | bytes 393224 | tf_op jit(solution)/shard_map/project/ppermute | solution.py:57
  123.0 2.4 %collective-permute-start.14 = (bf16[128,1024]{1,0:T(8,128)(2,1)S(1)}, bf16[128,1024]{1,0:T(8,128)(2,1)S(1)}, u32[]{:S(2)}, u32[]{:S(2)}) collective-permute-start(bf16[128,1024]{1,0:T(8,128)(2,1)S(1)} %depth.2.a_ref), channel_id=1, source_target_pairs={{0,4},{2,6},{4,0},{6,2},{1,5},{3,7},{5,1},{7,3},{8,12},{10,14},{12... | collective-permute-start | bytes 786440 | tf_op jit(solution)/shard_map/depth/ppermute | solution.py:39
  127.4 3.3 %all-to-all-start.4 = ((bf16[8,16,128]{2,1,0:T(8,128)(2,1)}), bf16[8,16,128]{2,1,0:T(8,128)(2,1)S(1)}, u32[]{:S(2)}, u32[]{:S(2)}) async-start(bf16[8,16,128]{2,1,0:T(8,128)(2,1)} %reshape.224), calls=%async_computation.4 | async-start | bytes 65536 | tf_op jit(solution)/shard_map/place_outputs/all_to_all | solution.py:27
  131.2 5.9 %collective-permute-done.14.c_ref = bf16[128,1024]{1,0:T(8,128)(2,1)S(1)} collective-permute-done((bf16[128,1024]{1,0:T(8,128)(2,1)S(1)}, bf16[128,1024]{1,0:T(8,128)(2,1)S(1)}, u32[]{:S(2)}, u32[]{:S(2)}) %collective-permute-start.14) | collective-permute-done | bytes 262176 | tf_op jit(solution)/shard_map/depth/ppermute | solution.py:39
  137.1 2.3 %copy-done.3 = bf16[2304,1024]{1,0:T(8,128)(2,1)S(1)} copy-done((bf16[2304,1024]{1,0:T(8,128)(2,1)S(1)}, bf16[2304,1024]{1,0:T(8,128)(2,1)}, u32[]{:S(2)}) %copy-start.3) | copy-done | bytes 4718616
  139.5 2.8 %depth.3 = bf16[8,4,32,128]{3,2,1,0:T(8,128)(2,1)} custom-call(bf16[128,1024]{1,0:T(8,128)(2,1)S(1)} %depth.2.a_ref, bf16[128,1024]{1,0:T(8,128)(2,1)S(1)} %collective-permute-done.13.b_ref, bf16[128,1024]{1,0:T(8,128)(2,1)S(1)} %collective-permute-done.14.c_ref, bf16[128,1024]{1,0:T(8,128)(2,1)S(1)} %collective-permute-done.15.d_ref, ...), custom_call_target="tpu_custom_call" | custom-call | flops 603979776 | bytes 5769216 | tf_op jit(solution)/shard_map/depth/pallas_call | solution.py:69
  142.3 6.4 %all-to-all-start.5 = ((bf16[64,16,128]{2,1,0:T(8,128)(2,1)}), bf16[64,16,128]{2,1,0:T(8,128)(2,1)S(1)}, u32[]{:S(2)}, u32[]{:S(2)}) async-start(bf16[64,16,128]{2,1,0:T(8,128)(2,1)} %bitcast.76), calls=%async_computation.5 | async-start | bytes 524288 | tf_op jit(solution)/shard_map/depth/all_to_all | solution.py:27
  149.5 12.3 %all-to-all-done.5 = bf16[64,16,128]{2,1,0:T(8,128)(2,1)S(1)} async-done(((bf16[64,16,128]{2,1,0:T(8,128)(2,1)}), bf16[64,16,128]{2,1,0:T(8,128)(2,1)S(1)}, u32[]{:S(2)}, u32[]{:S(2)}) %all-to-all-start.5) | async-done | bytes 262176 | tf_op jit(solution)/shard_map/depth/all_to_all | solution.py:27
  (160 shorter events, 34.5 us)
Async XLA Ops:
  7.2 72.0 %all-gather.5.cloned.1.call-start = ((), (), s32[]{:S(2)}) async-start(), calls=%async_computation.6 | async-start | bytes 3538944 | tf_op jit(solution)/shard_map/pack_weights/all_gather | solution.py:217
  8.4 4.3 %collective-permute-start.7 = (bf16[64,1024]{1,0:T(8,128)(2,1)S(1)}, bf16[64,1024]{1,0:T(8,128)(2,1)S(1)}, u32[]{:S(2)}, u32[]{:S(2)}) collective-permute-start(bf16[64,1024]{1,0:T(8,128)(2,1)S(1)} %get-tuple-element.37), channel_id=1, source_target_pairs={{0,1},{1,0},{2,3},{3,2},{4,5},{5,4},{6,7},{7,6},{8,9},{9,8},{10,11... | collective-permute-start | bytes 393224 | tf_op jit(solution)/shard_map/pack_weights/ppermute | solution.py:57
  17.1 24.0 %all-to-all-start = ((bf16[16,88,128]{2,1,0:T(8,128)(2,1)}), bf16[16,88,128]{2,1,0:T(8,128)(2,1)S(1)}, u32[]{:S(2)}, u32[]{:S(2)}) async-start(bf16[16,88,128]{2,1,0:T(8,128)(2,1)} %bitcast.4), calls=%async_computation | async-start | bytes 720896 | tf_op jit(solution)/shard_map/gather_hidden/all_to_all | solution.py:27
  24.2 112.9 %all-gather.7.cloned.1.call-start = ((), (), s32[]{:S(2)}) async-start(), calls=%async_computation.7 | async-start | bytes 5308416 | tf_op jit(solution)/shard_map/pack_weights/all_gather | solution.py:218
  24.2 35.1 %collective-permute-start.6 = (bf16[192,4096]{1,0:T(8,128)(2,1)}, bf16[192,4096]{1,0:T(8,128)(2,1)}, u32[]{:S(2)}, u32[]{:S(2)}) collective-permute-start(bf16[192,4096]{1,0:T(8,128)(2,1)} %bitcast.186), channel_id=1, source_target_pairs={{0,1},{1,0},{2,3},{3,2},{4,5},{5,4},{6,7},{7,6},{8,9},{9,8},{10,11... | collective-permute-start | bytes 4718600 | tf_op jit(solution)/shard_map/norm/ppermute | solution.py:57
  25.4 3.0 %collective-permute-start.16 = (bf16[144,1024]{1,0:T(8,128)(2,1)}, bf16[144,1024]{1,0:T(8,128)(2,1)S(1)}, u32[]{:S(2)}, u32[]{:S(2)}) collective-permute-start(bf16[144,1024]{1,0:T(8,128)(2,1)} %fusion.19), channel_id=1, source_target_pairs={{0,1},{1,0},{2,3},{3,2},{4,5},{5,4},{6,7},{7,6},{8,9},{9,8},{10,11... | collective-permute-start | bytes 884744 | tf_op jit(solution)/shard_map/pack_weights/ppermute | solution.py:57
  41.1 6.8 %collective-permute-start = (bf16[4,2,72,128]{3,2,1,0:T(8,128)(2,1)S(1)}, bf16[4,2,72,128]{3,2,1,0:T(8,128)(2,1)S(1)}, u32[]{:S(2)}, u32[]{:S(2)}) collective-permute-start(bf16[4,2,72,128]{3,2,1,0:T(8,128)(2,1)S(1)} %get-tuple-element.34), channel_id=1, source_target_pairs={{0,2},{2,4},{4,6},{6,0},{1,3},{3,5},{5,7},{7,1},{8,10},{10,12},{12... | collective-permute-start | bytes 442376 | tf_op jit(solution)/shard_map/norm/ppermute | solution.py:47
  42.5 11.7 %collective-permute-start.2 = (bf16[4,2,72,128]{3,2,1,0:T(8,128)(2,1)S(1)}, bf16[4,2,72,128]{3,2,1,0:T(8,128)(2,1)S(1)}, u32[]{:S(2)}, u32[]{:S(2)}) collective-permute-start(bf16[4,2,72,128]{3,2,1,0:T(8,128)(2,1)S(1)} %get-tuple-element.34), channel_id=1, source_target_pairs={{0,6},{2,0},{4,2},{6,4},{1,7},{3,1},{5,3},{7,5},{8,14},{10,8},{12,... | collective-permute-start | bytes 442376 | tf_op jit(solution)/shard_map/norm/ppermute | solution.py:50
  44.2 7.3 %collective-permute-start.3 = (bf16[4,2,72,128]{3,2,1,0:T(8,128)(2,1)S(1)}, bf16[4,2,72,128]{3,2,1,0:T(8,128)(2,1)S(1)}, u32[]{:S(2)}, u32[]{:S(2)}) collective-permute-start(bf16[4,2,72,128]{3,2,1,0:T(8,128)(2,1)S(1)} %get-tuple-element.35), channel_id=1, source_target_pairs={{0,6},{2,0},{4,2},{6,4},{1,7},{3,1},{5,3},{7,5},{8,14},{10,8},{12,... | collective-permute-start | bytes 442376 | tf_op jit(solution)/shard_map/norm/ppermute | solution.py:48
  45.5 8.8 %collective-permute-start.1 = (bf16[4,2,72,128]{3,2,1,0:T(8,128)(2,1)S(1)}, bf16[4,2,72,128]{3,2,1,0:T(8,128)(2,1)S(1)}, u32[]{:S(2)}, u32[]{:S(2)}) collective-permute-start(bf16[4,2,72,128]{3,2,1,0:T(8,128)(2,1)S(1)} %get-tuple-element.35), channel_id=1, source_target_pairs={{0,2},{2,4},{4,6},{6,0},{1,3},{3,5},{5,7},{7,1},{8,10},{10,12},{12... | collective-permute-start | bytes 442376 | tf_op jit(solution)/shard_map/norm/ppermute | solution.py:49
  47.9 9.6 %collective-permute-start.4 = (bf16[4,2,72,128]{3,2,1,0:T(8,128)(2,1)S(1)}, bf16[4,2,72,128]{3,2,1,0:T(8,128)(2,1)S(1)}, u32[]{:S(2)}, u32[]{:S(2)}) collective-permute-start(bf16[4,2,72,128]{3,2,1,0:T(8,128)(2,1)S(1)} %collective-permute-done), channel_id=1, source_target_pairs={{0,2},{2,4},{4,6},{6,0},{1,3},{3,5},{5,7},{7,1},{8,10},{10,12},{12... | collective-permute-start | bytes 442376 | tf_op jit(solution)/shard_map/norm/ppermute | solution.py:51
  51.5 5.9 %collective-permute-start.5 = (bf16[4,2,72,128]{3,2,1,0:T(8,128)(2,1)S(1)}, bf16[4,2,72,128]{3,2,1,0:T(8,128)(2,1)S(1)}, u32[]{:S(2)}, u32[]{:S(2)}) collective-permute-start(bf16[4,2,72,128]{3,2,1,0:T(8,128)(2,1)S(1)} %collective-permute-done.3), channel_id=1, source_target_pairs={{0,6},{2,0},{4,2},{6,4},{1,7},{3,1},{5,3},{7,5},{8,14},{10,8},{12,... | collective-permute-start | bytes 442376 | tf_op jit(solution)/shard_map/norm/ppermute | solution.py:52
  63.2 15.9 %all-to-all-start.1 = ((bf16[32,4,512]{2,1,0:T(4,128)(2,1)}), bf16[32,4,512]{2,1,0:T(4,128)(2,1)S(1)}, u32[]{:S(2)}, u32[]{:S(2)}) async-start(bf16[32,4,512]{2,1,0:T(4,128)(2,1)} %pad_maximum_fusion.4), calls=%async_computation.1 | async-start | bytes 262144 | tf_op jit(solution)/shard_map/qkv/all_to_all | solution.py:27
  102.7 10.2 %all-to-all-start.3 = ((bf16[8,128,128]{2,1,0:T(8,128)(2,1)}), bf16[8,128,128]{2,1,0:T(8,128)(2,1)S(1)}, u32[]{:S(2)}, u32[]{:S(2)}) async-start(bf16[8,128,128]{2,1,0:T(8,128)(2,1)} %project.1), calls=%async_computation.3 | async-start | bytes 524288 | tf_op jit(solution)/shard_map/project/all_to_all | solution.py:27
  106.4 6.9 %collective-permute-start.12 = (bf16[8,2,16,128]{3,2,1,0:T(8,128)(2,1)S(1)}, bf16[8,2,16,128]{3,2,1,0:T(8,128)(2,1)S(1)}, u32[]{:S(2)}, u32[]{:S(2)}) collective-permute-start(bf16[8,2,16,128]{3,2,1,0:T(8,128)(2,1)S(1)} %slice.166), channel_id=1, source_target_pairs={{0,64},{64,128},{128,192},{192,0},{2,66},{66,130},{130,194},{194,2... | collective-permute-start | bytes 196616 | tf_op jit(solution)/shard_map/embed/ppermute | solution.py:254
  113.0 4.5 %collective-permute-start.8 = (bf16[128,128]{1,0:T(8,128)(2,1)S(1)}, bf16[128,128]{1,0:T(8,128)(2,1)S(1)}, u32[]{:S(2)}, u32[]{:S(2)}) collective-permute-start(bf16[128,128]{1,0:T(8,128)(2,1)S(1)} %get-tuple-element.29), channel_id=1, source_target_pairs={{0,64},{64,128},{128,192},{192,0},{1,65},{65,129},{129,193},{193,1... | collective-permute-start | bytes 98312 | tf_op jit(solution)/shard_map/project/ppermute | solution.py:39
  113.4 4.7 %collective-permute-start.9 = (bf16[128,128]{1,0:T(8,128)(2,1)S(1)}, bf16[128,128]{1,0:T(8,128)(2,1)S(1)}, u32[]{:S(2)}, u32[]{:S(2)}) collective-permute-start(bf16[128,128]{1,0:T(8,128)(2,1)S(1)} %get-tuple-element.29), channel_id=1, source_target_pairs={{0,128},{64,192},{128,0},{192,64},{1,129},{65,193},{129,1},{193,65... | collective-permute-start | bytes 98312 | tf_op jit(solution)/shard_map/project/ppermute | solution.py:39
  115.2 3.3 %collective-permute-start.10 = (bf16[128,128]{1,0:T(8,128)(2,1)S(1)}, bf16[128,128]{1,0:T(8,128)(2,1)S(1)}, u32[]{:S(2)}, u32[]{:S(2)}) collective-permute-start(bf16[128,128]{1,0:T(8,128)(2,1)S(1)} %get-tuple-element.29), channel_id=1, source_target_pairs={{0,192},{64,0},{128,64},{192,128},{1,193},{65,1},{129,65},{193,129... | collective-permute-start | bytes 98312 | tf_op jit(solution)/shard_map/project/ppermute | solution.py:39
  118.5 3.1 %collective-permute-start.11 = (bf16[4,128,128]{2,1,0:T(8,128)(2,1)S(1)}, bf16[4,128,128]{2,1,0:T(8,128)(2,1)S(1)}, u32[]{:S(2)}, u32[]{:S(2)}) collective-permute-start(bf16[4,128,128]{2,1,0:T(8,128)(2,1)S(1)} %bitcast_dynamic-update-slice_fusion.own_ref), channel_id=1, source_target_pairs={{0,1},{1,0},{2,3},{3,2},{4,5},{5,4},{6,7},{7,6},{8,9},{9,8},{10,11... | collective-permute-start | bytes 393224 | tf_op jit(solution)/shard_map/project/ppermute | solution.py:57
  122.4 8.8 %collective-permute-start.13 = (bf16[128,1024]{1,0:T(8,128)(2,1)S(1)}, bf16[128,1024]{1,0:T(8,128)(2,1)S(1)}, u32[]{:S(2)}, u32[]{:S(2)}) collective-permute-start(bf16[128,1024]{1,0:T(8,128)(2,1)S(1)} %depth.2.a_ref), channel_id=1, source_target_pairs={{0,2},{2,4},{4,6},{6,0},{1,3},{3,5},{5,7},{7,1},{8,10},{10,12},{12... | collective-permute-start | bytes 786440 | tf_op jit(solution)/shard_map/depth/ppermute | solution.py:39
  123.0 14.1 %collective-permute-start.14 = (bf16[128,1024]{1,0:T(8,128)(2,1)S(1)}, bf16[128,1024]{1,0:T(8,128)(2,1)S(1)}, u32[]{:S(2)}, u32[]{:S(2)}) collective-permute-start(bf16[128,1024]{1,0:T(8,128)(2,1)S(1)} %depth.2.a_ref), channel_id=1, source_target_pairs={{0,4},{2,6},{4,0},{6,2},{1,5},{3,7},{5,1},{7,3},{8,12},{10,14},{12... | collective-permute-start | bytes 786440 | tf_op jit(solution)/shard_map/depth/ppermute | solution.py:39
  125.4 11.7 %collective-permute-start.15 = (bf16[128,1024]{1,0:T(8,128)(2,1)S(1)}, bf16[128,1024]{1,0:T(8,128)(2,1)S(1)}, u32[]{:S(2)}, u32[]{:S(2)}) collective-permute-start(bf16[128,1024]{1,0:T(8,128)(2,1)S(1)} %depth.2.a_ref), channel_id=1, source_target_pairs={{0,6},{2,0},{4,2},{6,4},{1,7},{3,1},{5,3},{7,5},{8,14},{10,8},{12,... | collective-permute-start | bytes 786440 | tf_op jit(solution)/shard_map/depth/ppermute | solution.py:39
  127.4 14.8 %all-to-all-start.4 = ((bf16[8,16,128]{2,1,0:T(8,128)(2,1)}), bf16[8,16,128]{2,1,0:T(8,128)(2,1)S(1)}, u32[]{:S(2)}, u32[]{:S(2)}) async-start(bf16[8,16,128]{2,1,0:T(8,128)(2,1)} %reshape.224), calls=%async_computation.4 | async-start | bytes 65536 | tf_op jit(solution)/shard_map/place_outputs/all_to_all | solution.py:27
  142.3 19.6 %all-to-all-start.5 = ((bf16[64,16,128]{2,1,0:T(8,128)(2,1)}), bf16[64,16,128]{2,1,0:T(8,128)(2,1)S(1)}, u32[]{:S(2)}, u32[]{:S(2)}) async-start(bf16[64,16,128]{2,1,0:T(8,128)(2,1)} %bitcast.76), calls=%async_computation.5 | async-start | bytes 524288 | tf_op jit(solution)/shard_map/depth/all_to_all | solution.py:27
  (13 other events, 152.6 us)
Sparse Core Ops, SparseCore 0:
  13.7 51.7 all-gather.4
  67.3 59.1 all-gather.6

commit v3 on v2

--- a/solution.py
+++ b/solution.py
@@ -116,6 +116,34 @@
         ],
         compiler_params=pltpu.CompilerParams(vmem_limit_bytes=24 * 1024 * 1024),
     )(hid_t, emb_t, token)
+
+
+def qkv_kernel(*refs):
+    part_refs, (own_ref, oth_ref, hid_ref, out_ref) = refs[:8], refs[8:]
+    yi, ci = lax.axis_index("y"), lax.axis_index("core")
+    squares = jnp.zeros((1, 128), F32)
+    sums = [jnp.zeros((192, 128), F32), jnp.zeros((192, 128), F32)]
+    for index, step in enumerate((0, 3, 1, 2)):
+        at = lax.rem(yi + step, Y)
+        gains = part_refs[2 * index][512:528].astype(F32)
+        for z in range(Z):
+            rows = pl.ds((z % 4) * 128, 128)
+            block = part_refs[2 * index + z // 4][rows]
+            wide = block.astype(F32)
+            squares += jnp.sum(wide * wide, axis=0, keepdims=True)
+            columns = pl.ds(pl.multiple_of(z * 512 + at * 128, 128), 128)
+            for which, w_ref in enumerate((own_ref, oth_ref)):
+                w = (w_ref[:, columns].astype(F32) * gains[z : z + 1]).astype(BF)
+                sums[which] += jnp.dot(w, block, preferred_element_type=F32)
+    inv = lax.rsqrt(squares / D + eps)
+    own, oth = sums[0] * inv, sums[1] * inv
+    low = jnp.where(ci == 0, own, oth)
+    high = jnp.where(ci == 0, oth, own)
+    pieces = []
+    for i in range(3):
+        pieces += [low[i * 64 : (i + 1) * 64], high[i * 64 : (i + 1) * 64]]
+    pieces.append(hid_ref[...].astype(F32))
+    out_ref[...] = jnp.concatenate(pieces, axis=0).T.astype(BF)
 
 
 def project_kernel(moved_ref, w_ref, out_ref):
@@ -220,33 +248,19 @@
     with jax.named_scope("norm"):
         w_own = w_qkv.transpose(0, 2, 1).reshape(192, D)
         w_oth = swap(w_own)
-        halves = (column[:4, :, :72], column[4:, :, :72])
-        pieces = [(halves, 0)] + list(zip(ring_halves(*halves, "y"), (3, 1, 2)))
-        blocks = [
-            (part, index * 4, lax.rem(yi + step, Y))
-            for parts, step in pieces
-            for index, part in enumerate(parts)
-        ]
-        sum_sq = sum(
-            jnp.sum(jnp.square(part[:, :, :64].astype(F32)), axis=(0, 1, 2))
-            for part, _, _ in blocks
-        )
-        inv = lax.rsqrt(sum_sq / D + eps)
-        normed = jnp.zeros((Z, Y, C, 64, 128), BF)
-        for part, at_z, at_y in blocks:
-            gain = part[:, :, 64, :64].astype(F32)[..., None]
-            block = (part[:, :, :64].astype(F32) * inv * gain).astype(BF)
-            normed = lax.dynamic_update_slice(normed, block[:, None], (at_z, at_y, 0, 0, 0))
-        normed = normed.reshape(D, 128)
+        gains = jnp.pad(column[:, :, 64, :64].reshape(Z, 128), ((0, 8), (0, 0)))
+        low = jnp.concatenate([column[:4, :, :64].reshape(512, 128), gains], axis=0)
+        high = column[4:, :, :64].reshape(512, 128)
+        others = ring_halves(low, high, "y")
 
     with jax.named_scope("qkv"):
-        q_own = jnp.einsum("dr,nd->rn", normed, w_own, preferred_element_type=F32).astype(BF)
-        q_oth = jnp.einsum("dr,nd->rn", normed, w_oth, preferred_element_type=F32).astype(BF)
-        q_low = jnp.where(ci == 0, q_own, q_oth).reshape(128, 3, 64)
-        q_high = jnp.where(ci == 0, q_oth, q_own).reshape(128, 3, 64)
-        hid_cols = pick(column, zi)[:, :64]
-        qkv = jnp.concatenate([q_low, q_high], axis=2).reshape(128, 384)
-        sent = jnp.concatenate([qkv, hid_cols.reshape(128, 128).T], axis=1)
+        hid_cols = pick(column, zi)[:, :64].reshape(128, 128)
+        sent = in_vmem(
+            qkv_kernel,
+            (128, 512),
+            2 * 128 * 384 * D,
+            (low, high, *others[0], *others[1], *others[2], w_own, w_oth, hid_cols),
+        )
         got = exchange(sent.reshape(32, 4, 512), ("z", "y"))
         got = got.reshape(HEADS, 4, 4, HEAD_DIM).transpose(1, 2, 0, 3)
 
@@ -304,6 +318,9 @@
         x_part = in_vmem(
             depth_in_kernel, (128, DD), 2 * 128 * 1024 * DD, (frame, frame_oth, first, emb)
         )
+        rows = lax.dynamic_slice_in_dim(frame, xi * 32, 32, 1)
+        rows = rows.reshape(X, 2, 16, 2, 64).transpose(0, 3, 2, 1, 4).reshape(Z, 16, 128)
+        rows, second = lax.optimization_barrier((rows, second))
         gain_d = lax.dynamic_slice_in_dim(depth_gain, ci, 1, 0).astype(F32)
         out = in_vmem(
             depth_ff_kernel,
@@ -317,8 +334,6 @@
     with jax.named_scope("place_outputs"):
         depth_out = out.reshape(Z, C, 16, X, 32).transpose(1, 3, 0, 4, 2)
         depth_out = depth_out.reshape(C, 1024, 16)
-        rows = lax.dynamic_slice_in_dim(frame, xi * 32, 32, 1)
-        rows = rows.reshape(X, 2, 16, 2, 64).transpose(0, 3, 2, 1, 4).reshape(Z, 16, 128)
         rows = exchange(rows, "z")
         temporal_out = rows.reshape(Z, 16, 2, 64).transpose(0, 2, 1, 3).reshape(256, 64)
     return (temporal_out, depth_out)

time: 171 us -> 169 us (0.988)
  blocking collectives: 15.5 us -> 39.1 us
  waiting for transfers between devices: 59.1 us -> 44 us
  starting transfers between devices: 48.8 us -> 41.3 us
  other arithmetic: 6.16 us -> 3.19 us
  matrix products: 6.44 us -> 3.88 us
  Pallas kernels: 5.32 us -> 7.87 us
    all_to_all x1 -> x2, blocking collectives: 15.5 us -> 39.1 us  [exchange(): return lax.all_to_all(value, axis, split_axis=0, concat_axis=0, tiled=True)]
    all_to_all x5 -> x4, waiting for transfers between devices: 39 us -> 26.7 us  [exchange(): return lax.all_to_all(value, axis, split_axis=0, concat_axis=0, tiled=True)]
    all_to_all x5 -> x4, starting transfers between devices: 27.2 us -> 18.1 us  [exchange(): return lax.all_to_all(value, axis, split_axis=0, concat_axis=0, tiled=True)]
    ppermute x1, waiting for transfers between devices: 0.01 us -> 5.97 us  [ring_halves(): high_behind = lax.ppermute(high, axis, up)]
    ppermute x1, waiting for transfers between devices: 3.43 us -> 0.01 us  [ring_halves(): high_ahead = lax.ppermute(high, axis, down)]
    ppermute x1, waiting for transfers between devices: 2.91 us -> 0.01 us  [ring_halves(): high_across = lax.ppermute(high_ahead, axis, down)]
    dot_general x2 -> x0, matrix products: 2.56 us -> none  [the longest x1 1.98 us: per_device(): jnp.einsum('dr,nd->rn', normed, w_oth, preferred_element_type=F32)]
    pallas_call x3 -> x4, Pallas kernels: 4.75 us -> 7.3 us  [in_vmem(): pl.pallas_call(kernel, in_specs=[pl.BlockSpec(memory_space=pltpu.VMEM)] *...]
  transfers between devices with their start and end apart: 24 -> 23, of which waited for: 15 -> 13; matrix products, arithmetic and copies ran while one was open for 10% -> 7% of each run, Pallas kernels for 3% -> 5%
where the time goes in v3:
time: 169 us; the launch traced here: 168 us
  waiting for transfers between devices  44 us (26%)
  starting transfers between devices  41.3 us (24%)
  blocking collectives  39.1 us (23%)
  between operations  14.7 us (9%)
  local copies, waits for them, and re-layouts  14.4 us (9%)
  Pallas kernels  7.87 us (5%)
  matrix products  3.88 us (2%)
  other arithmetic  3.19 us (2%)
    all_to_all x2, blocking collectives, exchange(): return lax.all_to_all(value, axis, split_axis=0, concat_axis=0, tiled=True)  39.1 us
    all_to_all x4, waiting for transfers between devices, exchange(): return lax.all_to_all(value, axis, split_axis=0, concat_axis=0, tiled=True)  26.7 us
    all_to_all x4, starting transfers between devices, exchange(): return lax.all_to_all(value, axis, split_axis=0, concat_axis=0, tiled=True)  18.1 us
    ppermute x6, starting transfers between devices, from_each(): lax.ppermute(value, axis, [(i, (i + step) % count) for i in range(count)])  8.28 us
    unnamed x36, local copies, waits for them, and re-layouts  7.3 us
    pallas_call x4, Pallas kernels, in_vmem(): pl.pallas_call(kernel, in_specs=[pl.BlockSpec(memory_space=pltpu.VMEM)] *...  7.3 us
    ppermute x6, waiting for transfers between devices, from_each(): lax.ppermute(value, axis, [(i, (i + step) % count) for i in range(count)])  6.48 us
    ppermute x4, starting transfers between devices, swap(): return lax.ppermute(value, 'core', [(0, 1), (1, 0)])  6.38 us
  transfers between devices with their start and end apart: 23, of which 13 were waited for; matrix products, arithmetic and copies ran while one was open for 7% of the time, Pallas kernels for 5%

profile of v3, /device:TPU:1, one launch (start us, length us, event | category | flops | bytes accessed | tf_op | source)
XLA Modules:
  0.0 168.4 jit_solution(9573987546496407341)
XLA Ops:
  8.4 3.3 %collective-permute-start.7 = (bf16[64,1024]{1,0:T(8,128)(2,1)S(1)}, bf16[64,1024]{1,0:T(8,128)(2,1)S(1)}, u32[]{:S(2)}, u32[]{:S(2)}) collective-permute-start(bf16[64,1024]{1,0:T(8,128)(2,1)S(1)} %get-tuple-element.39), channel_id=1, source_target_pairs={{0,1},{1,0},{2,3},{3,2},{4,5},{5,4},{6,7},{7,6},{8,9},{9,8},{10,11... | collective-permute-start | bytes 393224 | tf_op jit(solution)/shard_map/pack_weights/ppermute | solution.py:57
  17.7 23.8 %all_to_all.30 = bf16[16,88,128]{2,1,0:T(8,128)(2,1)S(1)} all-to-all(bf16[16,88,128]{2,1,0:T(8,128)(2,1)S(1)} %bitcast.119), channel_id=1, replica_groups=mesh['cb'=4,'z'=8,'y'=4,'core'=2] {'z','core'}, dimensions={0} | all-to-all | bytes 720896 | tf_op jit(solution)/shard_map/gather_hidden/all_to_all | solution.py:27
  42.9 1.7 collective-permute-start.3
  46.0 2.1 %collective-permute-done.refs_2_ = bf16[528,128]{1,0:T(8,128)(2,1)S(1)} collective-permute-done((bf16[528,128]{1,0:T(8,128)(2,1)S(1)}, bf16[528,128]{1,0:T(8,128)(2,1)S(1)}, u32[]{:S(2)}, u32[]{:S(2)}) %collective-permute-start) | collective-permute-done | bytes 135200 | tf_op jit(solution)/shard_map/norm/ppermute | solution.py:47
  49.7 1.8 %collective-permute-start.5 = (bf16[512,128]{1,0:T(8,128)(2,1)S(1)}, bf16[512,128]{1,0:T(8,128)(2,1)S(1)}, u32[]{:S(2)}, u32[]{:S(2)}) collective-permute-start(bf16[512,128]{1,0:T(8,128)(2,1)S(1)} %collective-permute-done.3.refs_5_), channel_id=1, source_target_pairs={{0,6},{2,0},{4,2},{6,4},{1,7},{3,1},{5,3},{7,5},{8,14},{10,8},{12,... | collective-permute-start | bytes 393224 | tf_op jit(solution)/shard_map/norm/ppermute | solution.py:52
  51.5 6.0 %collective-permute-done.1.refs_3_ = bf16[512,128]{1,0:T(8,128)(2,1)S(1)} collective-permute-done((bf16[512,128]{1,0:T(8,128)(2,1)S(1)}, bf16[512,128]{1,0:T(8,128)(2,1)S(1)}, u32[]{:S(2)}, u32[]{:S(2)}) %collective-permute-start.1) | collective-permute-done | bytes 131104 | tf_op jit(solution)/shard_map/norm/ppermute | solution.py:49
  58.9 2.6 %qkv.1 = bf16[128,512]{1,0:T(8,128)(2,1)S(1)} custom-call(bf16[528,128]{1,0:T(8,128)(2,1)S(1)} %fusion.21.refs_0_, bf16[512,128]{1,0:T(8,128)(2,1)S(1)} %bitcast.107, bf16[528,128]{1,0:T(8,128)(2,1)S(1)} %collective-permute-done.refs_2_, bf16[512,128]{1,0:T(8,128)(2,1)S(1)} %collective-permute-done.1.refs_3_, ...), custom_call_target="tpu_custom_call" | custom-call | flops 402653184 | bytes 4243456 | tf_op jit(solution)/shard_map/qkv/pallas_call | solution.py:69
  62.2 3.8 %all-to-all-start.1 = ((bf16[32,4,512]{2,1,0:T(4,128)(2,1)}), bf16[32,4,512]{2,1,0:T(4,128)(2,1)S(1)}, u32[]{:S(2)}, u32[]{:S(2)}) async-start(bf16[32,4,512]{2,1,0:T(4,128)(2,1)} %reshape.130), calls=%async_computation.1 | async-start | bytes 262144 | tf_op jit(solution)/shard_map/qkv/all_to_all | solution.py:27
  66.1 9.3 %all-to-all-done.1 = bf16[32,4,512]{2,1,0:T(4,128)(2,1)S(1)} async-done(((bf16[32,4,512]{2,1,0:T(4,128)(2,1)}), bf16[32,4,512]{2,1,0:T(4,128)(2,1)S(1)}, u32[]{:S(2)}, u32[]{:S(2)}) %all-to-all-start.1) | async-done | bytes 131104 | tf_op jit(solution)/shard_map/qkv/all_to_all | solution.py:27
  75.6 2.8 %fusion.3 = f32[4,32,1,64]{3,2,1,0:T(1,128)S(1)} fusion(bf16[4,32,128,1]{2,1,0,3:T(8,128)(2,1)S(1)} %slice_bitcast_fusion.4, bf16[4,64,4096]{2,1,0:T(8,128)(2,1)} %param.17), kind=kOutput, calls=%fused_computation.3 | convolution fusion | flops 2097152 | bytes 2162688 | tf_op jit(solution)/shard_map/attend/rhe,rphe->rhp/dot_general | solution.py:284
  80.6 15.3 %all_to_all.31 = bf16[32,4,640]{2,1,0:T(4,128)(2,1)S(1)} all-to-all(bf16[32,4,640]{2,1,0:T(4,128)(2,1)S(1)} %pad_maximum_fusion.2), channel_id=1, replica_groups=mesh['cb'=4,'z'=8,'y'=4,'core'=2] {'cb','y','core'}, dimensions={0} | all-to-all | bytes 327680 | tf_op jit(solution)/shard_map/project/all_to_all | solution.py:27
  96.1 1.9 %copy-done.1 = bf16[1536,1024]{1,0:T(8,128)(2,1)S(1)} copy-done((bf16[1536,1024]{1,0:T(8,128)(2,1)S(1)}, bf16[1536,1024]{1,0:T(8,128)(2,1)}, u32[]{:S(2)}) %copy-start.1) | copy-done | bytes 3145752
  99.2 3.6 %all-to-all-start.3 = ((bf16[8,128,128]{2,1,0:T(8,128)(2,1)}), bf16[8,128,128]{2,1,0:T(8,128)(2,1)S(1)}, u32[]{:S(2)}, u32[]{:S(2)}) async-start(bf16[8,128,128]{2,1,0:T(8,128)(2,1)} %project.1), calls=%async_computation.3 | async-start | bytes 524288 | tf_op jit(solution)/shard_map/project/all_to_all | solution.py:27
  104.4 5.0 %all-to-all-done.3 = bf16[8,128,128]{2,1,0:T(8,128)(2,1)S(1)} async-done(((bf16[8,128,128]{2,1,0:T(8,128)(2,1)}), bf16[8,128,128]{2,1,0:T(8,128)(2,1)S(1)}, u32[]{:S(2)}, u32[]{:S(2)}) %all-to-all-start.3) | async-done | bytes 262176 | tf_op jit(solution)/shard_map/project/all_to_all | solution.py:27
  111.0 1.5 collective-permute-start.9
  114.0 1.4 collective-permute-done.9
  115.8 2.2 %collective-permute-start.12 = (bf16[4,128,128]{2,1,0:T(8,128)(2,1)S(1)}, bf16[4,128,128]{2,1,0:T(8,128)(2,1)S(1)}, u32[]{:S(2)}, u32[]{:S(2)}) collective-permute-start(bf16[4,128,128]{2,1,0:T(8,128)(2,1)S(1)} %bitcast_dynamic-update-slice_fusion.own_ref), channel_id=1, source_target_pairs={{0,1},{1,0},{2,3},{3,2},{4,5},{5,4},{6,7},{7,6},{8,9},{9,8},{10,11... | collective-permute-start | bytes 393224 | tf_op jit(solution)/shard_map/project/ppermute | solution.py:57
  121.1 2.4 %collective-permute-start.15 = (bf16[128,1024]{1,0:T(8,128)(2,1)S(1)}, bf16[128,1024]{1,0:T(8,128)(2,1)S(1)}, u32[]{:S(2)}, u32[]{:S(2)}) collective-permute-start(bf16[128,1024]{1,0:T(8,128)(2,1)S(1)} %depth.2.a_ref), channel_id=1, source_target_pairs={{0,4},{2,6},{4,0},{6,2},{1,5},{3,7},{5,1},{7,3},{8,12},{10,14},{12... | collective-permute-start | bytes 786440 | tf_op jit(solution)/shard_map/depth/ppermute | solution.py:39
  126.6 4.0 %all-to-all-start.4 = ((bf16[8,16,128]{2,1,0:T(8,128)(2,1)}), bf16[8,16,128]{2,1,0:T(8,128)(2,1)S(1)}, u32[]{:S(2)}, u32[]{:S(2)}) async-start(bf16[8,16,128]{2,1,0:T(8,128)(2,1)} %reshape.137), calls=%async_computation.4 | async-start | bytes 65536 | tf_op jit(solution)/shard_map/place_outputs/all_to_all | solution.py:27
  130.6 4.6 %collective-permute-done.15.c_ref = bf16[128,1024]{1,0:T(8,128)(2,1)S(1)} collective-permute-done((bf16[128,1024]{1,0:T(8,128)(2,1)S(1)}, bf16[128,1024]{1,0:T(8,128)(2,1)S(1)}, u32[]{:S(2)}, u32[]{:S(2)}) %collective-permute-start.15) | collective-permute-done | bytes 262176 | tf_op jit(solution)/shard_map/depth/ppermute | solution.py:39
  135.2 2.3 %copy-done.3 = bf16[2304,1024]{1,0:T(8,128)(2,1)S(1)} copy-done((bf16[2304,1024]{1,0:T(8,128)(2,1)S(1)}, bf16[2304,1024]{1,0:T(8,128)(2,1)}, u32[]{:S(2)}) %copy-start.3) | copy-done | bytes 4718616
  137.5 2.8 %depth.3 = bf16[8,4,32,128]{3,2,1,0:T(8,128)(2,1)} custom-call(bf16[128,1024]{1,0:T(8,128)(2,1)S(1)} %depth.2.a_ref, bf16[128,1024]{1,0:T(8,128)(2,1)S(1)} %collective-permute-done.14.b_ref, bf16[128,1024]{1,0:T(8,128)(2,1)S(1)} %collective-permute-done.15.c_ref, bf16[128,1024]{1,0:T(8,128)(2,1)S(1)} %collective-permute-done.16.d_ref, ...), custom_call_target="tpu_custom_call" | custom-call | flops 603979776 | bytes 5769216 | tf_op jit(solution)/shard_map/depth/pallas_call | solution.py:69
  140.4 6.6 %all-to-all-start.5 = ((bf16[64,16,128]{2,1,0:T(8,128)(2,1)}), bf16[64,16,128]{2,1,0:T(8,128)(2,1)S(1)}, u32[]{:S(2)}, u32[]{:S(2)}) async-start(bf16[64,16,128]{2,1,0:T(8,128)(2,1)} %bitcast.50), calls=%async_computation.5 | async-start | bytes 524288 | tf_op jit(solution)/shard_map/depth/all_to_all | solution.py:27
  147.8 12.3 %all-to-all-done.5 = bf16[64,16,128]{2,1,0:T(8,128)(2,1)S(1)} async-done(((bf16[64,16,128]{2,1,0:T(8,128)(2,1)}), bf16[64,16,128]{2,1,0:T(8,128)(2,1)S(1)}, u32[]{:S(2)}, u32[]{:S(2)}) %all-to-all-start.5) | async-done | bytes 262176 | tf_op jit(solution)/shard_map/depth/all_to_all | solution.py:27
  (138 shorter events, 30.5 us)
Async XLA Ops:
  7.2 72.1 %copy-start = (bf16[4,64,4096]{2,1,0:T(8,128)(2,1)S(1)}, bf16[4,64,4096]{2,1,0:T(8,128)(2,1)}, u32[]{:S(2)}) copy-start(bf16[4,64,4096]{2,1,0:T(8,128)(2,1)} %param.18) | copy-start | bytes 6291460
  7.2 68.4 %all-gather.5.cloned.1.call-start = ((), (), s32[]{:S(2)}) async-start(), calls=%async_computation.6 | async-start | bytes 3538944 | tf_op jit(solution)/shard_map/pack_weights/all_gather | solution.py:245
  8.4 4.3 %collective-permute-start.7 = (bf16[64,1024]{1,0:T(8,128)(2,1)S(1)}, bf16[64,1024]{1,0:T(8,128)(2,1)S(1)}, u32[]{:S(2)}, u32[]{:S(2)}) collective-permute-start(bf16[64,1024]{1,0:T(8,128)(2,1)S(1)} %get-tuple-element.39), channel_id=1, source_target_pairs={{0,1},{1,0},{2,3},{3,2},{4,5},{5,4},{6,7},{7,6},{8,9},{9,8},{10,11... | collective-permute-start | bytes 393224 | tf_op jit(solution)/shard_map/pack_weights/ppermute | solution.py:57
  13.5 113.0 %all-gather.7.cloned.1.call-start = ((), (), s32[]{:S(2)}) async-start(), calls=%async_computation.7 | async-start | bytes 5308416 | tf_op jit(solution)/shard_map/pack_weights/all_gather | solution.py:246
  13.9 1.7 collective-permute-start.11
  16.5 41.0 %collective-permute-start.6 = (bf16[192,4096]{1,0:T(8,128)(2,1)}, bf16[192,4096]{1,0:T(8,128)(2,1)}, u32[]{:S(2)}, u32[]{:S(2)}) collective-permute-start(bf16[192,4096]{1,0:T(8,128)(2,1)} %bitcast.103), channel_id=1, source_target_pairs={{0,1},{1,0},{2,3},{3,2},{4,5},{5,4},{6,7},{7,6},{8,9},{9,8},{10,11... | collective-permute-start | bytes 4718600 | tf_op jit(solution)/shard_map/norm/ppermute | solution.py:57
  41.6 6.5 %collective-permute-start = (bf16[528,128]{1,0:T(8,128)(2,1)S(1)}, bf16[528,128]{1,0:T(8,128)(2,1)S(1)}, u32[]{:S(2)}, u32[]{:S(2)}) collective-permute-start(bf16[528,128]{1,0:T(8,128)(2,1)S(1)} %fusion.21.refs_0_), channel_id=1, source_target_pairs={{0,2},{2,4},{4,6},{6,0},{1,3},{3,5},{5,7},{7,1},{8,10},{10,12},{12... | collective-permute-start | bytes 405512 | tf_op jit(solution)/shard_map/norm/ppermute | solution.py:47
  42.9 6.8 %collective-permute-start.3 = (bf16[512,128]{1,0:T(8,128)(2,1)S(1)}, bf16[512,128]{1,0:T(8,128)(2,1)S(1)}, u32[]{:S(2)}, u32[]{:S(2)}) collective-permute-start(bf16[512,128]{1,0:T(8,128)(2,1)S(1)} %bitcast.105), channel_id=1, source_target_pairs={{0,6},{2,0},{4,2},{6,4},{1,7},{3,1},{5,3},{7,5},{8,14},{10,8},{12,... | collective-permute-start | bytes 393224 | tf_op jit(solution)/shard_map/norm/ppermute | solution.py:48
  44.6 12.8 %collective-permute-start.2 = (bf16[528,128]{1,0:T(8,128)(2,1)S(1)}, bf16[528,128]{1,0:T(8,128)(2,1)S(1)}, u32[]{:S(2)}, u32[]{:S(2)}) collective-permute-start(bf16[528,128]{1,0:T(8,128)(2,1)S(1)} %fusion.21.refs_0_), channel_id=1, source_target_pairs={{0,6},{2,0},{4,2},{6,4},{1,7},{3,1},{5,3},{7,5},{8,14},{10,8},{12,... | collective-permute-start | bytes 405512 | tf_op jit(solution)/shard_map/norm/ppermute | solution.py:50
  48.1 9.4 %collective-permute-start.4 = (bf16[528,128]{1,0:T(8,128)(2,1)S(1)}, bf16[528,128]{1,0:T(8,128)(2,1)S(1)}, u32[]{:S(2)}, u32[]{:S(2)}) collective-permute-start(bf16[528,128]{1,0:T(8,128)(2,1)S(1)} %collective-permute-done.refs_2_), channel_id=1, source_target_pairs={{0,2},{2,4},{4,6},{6,0},{1,3},{3,5},{5,7},{7,1},{8,10},{10,12},{12... | collective-permute-start | bytes 405512 | tf_op jit(solution)/shard_map/norm/ppermute | solution.py:51
  48.3 9.2 %collective-permute-start.1 = (bf16[512,128]{1,0:T(8,128)(2,1)S(1)}, bf16[512,128]{1,0:T(8,128)(2,1)S(1)}, u32[]{:S(2)}, u32[]{:S(2)}) collective-permute-start(bf16[512,128]{1,0:T(8,128)(2,1)S(1)} %bitcast.106), channel_id=1, source_target_pairs={{0,2},{2,4},{4,6},{6,0},{1,3},{3,5},{5,7},{7,1},{8,10},{10,12},{12... | collective-permute-start | bytes 393224 | tf_op jit(solution)/shard_map/norm/ppermute | solution.py:49
  49.7 7.8 %collective-permute-start.5 = (bf16[512,128]{1,0:T(8,128)(2,1)S(1)}, bf16[512,128]{1,0:T(8,128)(2,1)S(1)}, u32[]{:S(2)}, u32[]{:S(2)}) collective-permute-start(bf16[512,128]{1,0:T(8,128)(2,1)S(1)} %collective-permute-done.3.refs_5_), channel_id=1, source_target_pairs={{0,6},{2,0},{4,2},{6,4},{1,7},{3,1},{5,3},{7,5},{8,14},{10,8},{12,... | collective-permute-start | bytes 393224 | tf_op jit(solution)/shard_map/norm/ppermute | solution.py:52
  62.2 13.3 %all-to-all-start.1 = ((bf16[32,4,512]{2,1,0:T(4,128)(2,1)}), bf16[32,4,512]{2,1,0:T(4,128)(2,1)S(1)}, u32[]{:S(2)}, u32[]{:S(2)}) async-start(bf16[32,4,512]{2,1,0:T(4,128)(2,1)} %reshape.130), calls=%async_computation.1 | async-start | bytes 262144 | tf_op jit(solution)/shard_map/qkv/all_to_all | solution.py:27
  99.2 10.2 %all-to-all-start.3 = ((bf16[8,128,128]{2,1,0:T(8,128)(2,1)}), bf16[8,128,128]{2,1,0:T(8,128)(2,1)S(1)}, u32[]{:S(2)}, u32[]{:S(2)}) async-start(bf16[8,128,128]{2,1,0:T(8,128)(2,1)} %project.1), calls=%async_computation.3 | async-start | bytes 524288 | tf_op jit(solution)/shard_map/project/all_to_all | solution.py:27
  103.8 6.1 %collective-permute-start.13 = (bf16[8,2,16,128]{3,2,1,0:T(8,128)(2,1)S(1)}, bf16[8,2,16,128]{3,2,1,0:T(8,128)(2,1)S(1)}, u32[]{:S(2)}, u32[]{:S(2)}) collective-permute-start(bf16[8,2,16,128]{3,2,1,0:T(8,128)(2,1)S(1)} %slice.87), channel_id=1, source_target_pairs={{0,64},{64,128},{128,192},{192,0},{2,66},{66,130},{130,194},{194,2... | collective-permute-start | bytes 196616 | tf_op jit(solution)/shard_map/embed/ppermute | solution.py:268
  109.5 4.5 %collective-permute-start.8 = (bf16[128,128]{1,0:T(8,128)(2,1)S(1)}, bf16[128,128]{1,0:T(8,128)(2,1)S(1)}, u32[]{:S(2)}, u32[]{:S(2)}) collective-permute-start(bf16[128,128]{1,0:T(8,128)(2,1)S(1)} %get-tuple-element.33), channel_id=1, source_target_pairs={{0,64},{64,128},{128,192},{192,0},{1,65},{65,129},{129,193},{193,1... | collective-permute-start | bytes 98312 | tf_op jit(solution)/shard_map/project/ppermute | solution.py:39
  111.0 4.4 %collective-permute-start.9 = (bf16[128,128]{1,0:T(8,128)(2,1)S(1)}, bf16[128,128]{1,0:T(8,128)(2,1)S(1)}, u32[]{:S(2)}, u32[]{:S(2)}) collective-permute-start(bf16[128,128]{1,0:T(8,128)(2,1)S(1)} %get-tuple-element.33), channel_id=1, source_target_pairs={{0,128},{64,192},{128,0},{192,64},{1,129},{65,193},{129,1},{193,65... | collective-permute-start | bytes 98312 | tf_op jit(solution)/shard_map/project/ppermute | solution.py:39
  112.5 3.3 %collective-permute-start.10 = (bf16[128,128]{1,0:T(8,128)(2,1)S(1)}, bf16[128,128]{1,0:T(8,128)(2,1)S(1)}, u32[]{:S(2)}, u32[]{:S(2)}) collective-permute-start(bf16[128,128]{1,0:T(8,128)(2,1)S(1)} %get-tuple-element.33), channel_id=1, source_target_pairs={{0,192},{64,0},{128,64},{192,128},{1,193},{65,1},{129,65},{193,129... | collective-permute-start | bytes 98312 | tf_op jit(solution)/shard_map/project/ppermute | solution.py:39
  115.8 3.1 %collective-permute-start.12 = (bf16[4,128,128]{2,1,0:T(8,128)(2,1)S(1)}, bf16[4,128,128]{2,1,0:T(8,128)(2,1)S(1)}, u32[]{:S(2)}, u32[]{:S(2)}) collective-permute-start(bf16[4,128,128]{2,1,0:T(8,128)(2,1)S(1)} %bitcast_dynamic-update-slice_fusion.own_ref), channel_id=1, source_target_pairs={{0,1},{1,0},{2,3},{3,2},{4,5},{5,4},{6,7},{7,6},{8,9},{9,8},{10,11... | collective-permute-start | bytes 393224 | tf_op jit(solution)/shard_map/project/ppermute | solution.py:57
  119.7 11.0 %collective-permute-start.14 = (bf16[128,1024]{1,0:T(8,128)(2,1)S(1)}, bf16[128,1024]{1,0:T(8,128)(2,1)S(1)}, u32[]{:S(2)}, u32[]{:S(2)}) collective-permute-start(bf16[128,1024]{1,0:T(8,128)(2,1)S(1)} %depth.2.a_ref), channel_id=1, source_target_pairs={{0,2},{2,4},{4,6},{6,0},{1,3},{3,5},{5,7},{7,1},{8,10},{10,12},{12... | collective-permute-start | bytes 786440 | tf_op jit(solution)/shard_map/depth/ppermute | solution.py:39
  121.1 14.1 %collective-permute-start.15 = (bf16[128,1024]{1,0:T(8,128)(2,1)S(1)}, bf16[128,1024]{1,0:T(8,128)(2,1)S(1)}, u32[]{:S(2)}, u32[]{:S(2)}) collective-permute-start(bf16[128,1024]{1,0:T(8,128)(2,1)S(1)} %depth.2.a_ref), channel_id=1, source_target_pairs={{0,4},{2,6},{4,0},{6,2},{1,5},{3,7},{5,1},{7,3},{8,12},{10,14},{12... | collective-permute-start | bytes 786440 | tf_op jit(solution)/shard_map/depth/ppermute | solution.py:39
  123.5 11.7 %collective-permute-start.16 = (bf16[128,1024]{1,0:T(8,128)(2,1)S(1)}, bf16[128,1024]{1,0:T(8,128)(2,1)S(1)}, u32[]{:S(2)}, u32[]{:S(2)}) collective-permute-start(bf16[128,1024]{1,0:T(8,128)(2,1)S(1)} %depth.2.a_ref), channel_id=1, source_target_pairs={{0,6},{2,0},{4,2},{6,4},{1,7},{3,1},{5,3},{7,5},{8,14},{10,8},{12,... | collective-permute-start | bytes 786440 | tf_op jit(solution)/shard_map/depth/ppermute | solution.py:39
  126.6 13.8 %all-to-all-start.4 = ((bf16[8,16,128]{2,1,0:T(8,128)(2,1)}), bf16[8,16,128]{2,1,0:T(8,128)(2,1)S(1)}, u32[]{:S(2)}, u32[]{:S(2)}) async-start(bf16[8,16,128]{2,1,0:T(8,128)(2,1)} %reshape.137), calls=%async_computation.4 | async-start | bytes 65536 | tf_op jit(solution)/shard_map/place_outputs/all_to_all | solution.py:27
  140.4 19.8 %all-to-all-start.5 = ((bf16[64,16,128]{2,1,0:T(8,128)(2,1)}), bf16[64,16,128]{2,1,0:T(8,128)(2,1)S(1)}, u32[]{:S(2)}, u32[]{:S(2)}) async-start(bf16[64,16,128]{2,1,0:T(8,128)(2,1)} %bitcast.50), calls=%async_computation.5 | async-start | bytes 524288 | tf_op jit(solution)/shard_map/depth/all_to_all | solution.py:27
  (14 other events, 77.2 us)
Sparse Core Ops, SparseCore 0:
  13.7 51.9 all-gather.4
  67.5 59.0 all-gather.6

commit v4 on v3

--- a/solution.py
+++ b/solution.py
@@ -265,10 +265,9 @@
         got = got.reshape(HEADS, 4, 4, HEAD_DIM).transpose(1, 2, 0, 3)
 
     with jax.named_scope("embed"):
-        moved_emb = lax.ppermute(
-            emb_here, ("cb", "core"), [(2 * x, 2 * ((x + 1) % X)) for x in range(X)]
-        )
-        emb = jnp.where(ci == 0, moved_emb, emb_here).reshape(256, 128)
+        pairs = [(2 * x, 2 * ((x + 1) % X)) for x in range(X)]
+        pairs += [(2 * x + 1, 2 * x + 1) for x in range(X)]
+        emb = lax.ppermute(emb_here, ("cb", "core"), pairs).reshape(256, 128)
         source = lax.broadcasted_iota(jnp.int32, (256, DD), 0)
         target = lax.broadcasted_iota(jnp.int32, (256, DD), 1)
         place = (target == (source // 32) * 128 + yi * 32 + source % 32).astype(BF)

time: 169 us -> 174 us (1.030)
  waiting for transfers between devices: 44 us -> 48 us
  local copies, waits for them, and re-layouts: 14.4 us -> 16.2 us
    ppermute x4, starting transfers between devices: 6.38 us -> 9.77 us  [swap(): return lax.ppermute(value, 'core', [(0, 1), (1, 0)])]
    ppermute x6, waiting for transfers between devices: 6.48 us -> 9.87 us  [from_each(): lax.ppermute(value, axis, [(i, (i + step) % count) for i in range(count)])]
    ppermute x6, starting transfers between devices: 8.28 us -> 6.11 us  [from_each(): lax.ppermute(value, axis, [(i, (i + step) % count) for i in range(count)])]
    unnamed x36, local copies, waits for them, and re-layouts: 7.3 us -> 9.18 us
  transfers between devices with their start and end apart: 23 -> 23, of which waited for: 13 -> 13; matrix products, arithmetic and copies ran while one was open for 7% -> 6% of each run, Pallas kernels for 5% -> 5%
where the time goes in v4:
time: 174 us; the launch traced here: 173 us
  waiting for transfers between devices  48 us (28%)
  starting transfers between devices  41.5 us (24%)
  blocking collectives  39.1 us (22%)
  local copies, waits for them, and re-layouts  16.2 us (9%)
  between operations  14.6 us (8%)
  Pallas kernels  7.84 us (5%)
  matrix products  3.88 us (2%)
  other arithmetic  2.07 us (1%)
    all_to_all x2, blocking collectives, exchange(): return lax.all_to_all(value, axis, split_axis=0, concat_axis=0, tiled=True)  39.1 us
    all_to_all x4, waiting for transfers between devices, exchange(): return lax.all_to_all(value, axis, split_axis=0, concat_axis=0, tiled=True)  28.2 us
    all_to_all x4, starting transfers between devices, exchange(): return lax.all_to_all(value, axis, split_axis=0, concat_axis=0, tiled=True)  17.1 us
    ppermute x6, waiting for transfers between devices, from_each(): lax.ppermute(value, axis, [(i, (i + step) % count) for i in range(count)])  9.87 us
    ppermute x4, starting transfers between devices, swap(): return lax.ppermute(value, 'core', [(0, 1), (1, 0)])  9.77 us
    unnamed x36, local copies, waits for them, and re-layouts  9.18 us
    pallas_call x4, Pallas kernels, in_vmem(): pl.pallas_call(kernel, in_specs=[pl.BlockSpec(memory_space=pltpu.VMEM)] *...  7.27 us
    ppermute x6, starting transfers between devices, from_each(): lax.ppermute(value, axis, [(i, (i + step) % count) for i in range(count)])  6.11 us
  transfers between devices with their start and end apart: 23, of which 13 were waited for; matrix products, arithmetic and copies ran while one was open for 6% of the time, Pallas kernels for 5%

profile of v4, /device:TPU:1, one launch (start us, length us, event | category | flops | bytes accessed | tf_op | source)
XLA Modules:
  0.0 173.2 jit_solution(3372836173174004328)
XLA Ops:
  8.4 3.3 %collective-permute-start.7 = (bf16[64,1024]{1,0:T(8,128)(2,1)S(1)}, bf16[64,1024]{1,0:T(8,128)(2,1)S(1)}, u32[]{:S(2)}, u32[]{:S(2)}) collective-permute-start(bf16[64,1024]{1,0:T(8,128)(2,1)S(1)} %get-tuple-element.39), channel_id=1, source_target_pairs={{0,1},{1,0},{2,3},{3,2},{4,5},{5,4},{6,7},{7,6},{8,9},{9,8},{10,11... | collective-permute-start | bytes 393224 | tf_op jit(solution)/shard_map/pack_weights/ppermute | solution.py:57
  17.7 23.8 %all_to_all.30 = bf16[16,88,128]{2,1,0:T(8,128)(2,1)S(1)} all-to-all(bf16[16,88,128]{2,1,0:T(8,128)(2,1)S(1)} %bitcast.118), channel_id=1, replica_groups=mesh['cb'=4,'z'=8,'y'=4,'core'=2] {'z','core'}, dimensions={0} | all-to-all | bytes 720896 | tf_op jit(solution)/shard_map/gather_hidden/all_to_all | solution.py:27
  46.0 2.1 %collective-permute-done.refs_2_ = bf16[528,128]{1,0:T(8,128)(2,1)S(1)} collective-permute-done((bf16[528,128]{1,0:T(8,128)(2,1)S(1)}, bf16[528,128]{1,0:T(8,128)(2,1)S(1)}, u32[]{:S(2)}, u32[]{:S(2)}) %collective-permute-start) | collective-permute-done | bytes 135200 | tf_op jit(solution)/shard_map/norm/ppermute | solution.py:47
  49.7 1.8 %collective-permute-start.5 = (bf16[512,128]{1,0:T(8,128)(2,1)S(1)}, bf16[512,128]{1,0:T(8,128)(2,1)S(1)}, u32[]{:S(2)}, u32[]{:S(2)}) collective-permute-start(bf16[512,128]{1,0:T(8,128)(2,1)S(1)} %collective-permute-done.3.refs_5_), channel_id=1, source_target_pairs={{0,6},{2,0},{4,2},{6,4},{1,7},{3,1},{5,3},{7,5},{8,14},{10,8},{12,... | collective-permute-start | bytes 393224 | tf_op jit(solution)/shard_map/norm/ppermute | solution.py:52
  51.5 6.0 %collective-permute-done.1.refs_3_ = bf16[512,128]{1,0:T(8,128)(2,1)S(1)} collective-permute-done((bf16[512,128]{1,0:T(8,128)(2,1)S(1)}, bf16[512,128]{1,0:T(8,128)(2,1)S(1)}, u32[]{:S(2)}, u32[]{:S(2)}) %collective-permute-start.1) | collective-permute-done | bytes 131104 | tf_op jit(solution)/shard_map/norm/ppermute | solution.py:49
  58.9 2.6 %qkv.1 = bf16[128,512]{1,0:T(8,128)(2,1)S(1)} custom-call(bf16[528,128]{1,0:T(8,128)(2,1)S(1)} %fusion.21.refs_0_, bf16[512,128]{1,0:T(8,128)(2,1)S(1)} %bitcast.107, bf16[528,128]{1,0:T(8,128)(2,1)S(1)} %collective-permute-done.refs_2_, bf16[512,128]{1,0:T(8,128)(2,1)S(1)} %collective-permute-done.1.refs_3_, ...), custom_call_target="tpu_custom_call" | custom-call | flops 402653184 | bytes 4243456 | tf_op jit(solution)/shard_map/qkv/pallas_call | solution.py:69
  62.2 3.8 %all-to-all-start.1 = ((bf16[32,4,512]{2,1,0:T(4,128)(2,1)}), bf16[32,4,512]{2,1,0:T(4,128)(2,1)S(1)}, u32[]{:S(2)}, u32[]{:S(2)}) async-start(bf16[32,4,512]{2,1,0:T(4,128)(2,1)} %reshape.130), calls=%async_computation.1 | async-start | bytes 262144 | tf_op jit(solution)/shard_map/qkv/all_to_all | solution.py:27
  66.1 9.3 %all-to-all-done.1 = bf16[32,4,512]{2,1,0:T(4,128)(2,1)S(1)} async-done(((bf16[32,4,512]{2,1,0:T(4,128)(2,1)}), bf16[32,4,512]{2,1,0:T(4,128)(2,1)S(1)}, u32[]{:S(2)}, u32[]{:S(2)}) %all-to-all-start.1) | async-done | bytes 131104 | tf_op jit(solution)/shard_map/qkv/all_to_all | solution.py:27
  75.6 2.8 %fusion.3 = f32[4,32,1,64]{3,2,1,0:T(1,128)S(1)} fusion(bf16[4,32,128,1]{2,1,0,3:T(8,128)(2,1)S(1)} %slice_bitcast_fusion.4, bf16[4,64,4096]{2,1,0:T(8,128)(2,1)} %param.17), kind=kOutput, calls=%fused_computation.3 | convolution fusion | flops 2097152 | bytes 2162688 | tf_op jit(solution)/shard_map/attend/rhe,rphe->rhp/dot_general | solution.py:283
  80.6 15.3 %all_to_all.31 = bf16[32,4,640]{2,1,0:T(4,128)(2,1)S(1)} all-to-all(bf16[32,4,640]{2,1,0:T(4,128)(2,1)S(1)} %pad_maximum_fusion.2), channel_id=1, replica_groups=mesh['cb'=4,'z'=8,'y'=4,'core'=2] {'cb','y','core'}, dimensions={0} | all-to-all | bytes 327680 | tf_op jit(solution)/shard_map/project/all_to_all | solution.py:27
  96.1 1.9 %copy-done.1 = bf16[1536,1024]{1,0:T(8,128)(2,1)S(1)} copy-done((bf16[1536,1024]{1,0:T(8,128)(2,1)S(1)}, bf16[1536,1024]{1,0:T(8,128)(2,1)}, u32[]{:S(2)}) %copy-start.1) | copy-done | bytes 3145752
  99.2 3.6 %all-to-all-start.3 = ((bf16[8,128,128]{2,1,0:T(8,128)(2,1)}), bf16[8,128,128]{2,1,0:T(8,128)(2,1)S(1)}, u32[]{:S(2)}, u32[]{:S(2)}) async-start(bf16[8,128,128]{2,1,0:T(8,128)(2,1)} %project.1), calls=%async_computation.3 | async-start | bytes 524288 | tf_op jit(solution)/shard_map/project/all_to_all | solution.py:27
  102.8 6.6 %all-to-all-done.3 = bf16[8,128,128]{2,1,0:T(8,128)(2,1)S(1)} async-done(((bf16[8,128,128]{2,1,0:T(8,128)(2,1)}), bf16[8,128,128]{2,1,0:T(8,128)(2,1)S(1)}, u32[]{:S(2)}, u32[]{:S(2)}) %all-to-all-start.3) | async-done | bytes 262176 | tf_op jit(solution)/shard_map/project/all_to_all | solution.py:27
  111.4 1.8 %collective-permute-start.9 = (bf16[128,128]{1,0:T(8,128)(2,1)S(1)}, bf16[128,128]{1,0:T(8,128)(2,1)S(1)}, u32[]{:S(2)}, u32[]{:S(2)}) collective-permute-start(bf16[128,128]{1,0:T(8,128)(2,1)S(1)} %get-tuple-element.33), channel_id=1, source_target_pairs={{0,128},{64,192},{128,0},{192,64},{1,129},{65,193},{129,1},{193,65... | collective-permute-start | bytes 98312 | tf_op jit(solution)/shard_map/project/ppermute | solution.py:39
  116.5 5.5 %collective-permute-start.12 = (bf16[4,128,128]{2,1,0:T(8,128)(2,1)S(1)}, bf16[4,128,128]{2,1,0:T(8,128)(2,1)S(1)}, u32[]{:S(2)}, u32[]{:S(2)}) collective-permute-start(bf16[4,128,128]{2,1,0:T(8,128)(2,1)S(1)} %bitcast_dynamic-update-slice_fusion.own_ref), channel_id=1, source_target_pairs={{0,1},{1,0},{2,3},{3,2},{4,5},{5,4},{6,7},{7,6},{8,9},{9,8},{10,11... | collective-permute-start | bytes 393224 | tf_op jit(solution)/shard_map/project/ppermute | solution.py:57
  123.0 1.9 %copy-done.2 = bf16[1536,1024]{1,0:T(8,128)(2,1)S(1)} copy-done((bf16[1536,1024]{1,0:T(8,128)(2,1)S(1)}, bf16[1536,1024]{1,0:T(8,128)(2,1)}, u32[]{:S(2)}) %copy-start.2) | copy-done | bytes 3145752
  126.0 1.8 %collective-permute-start.15 = (bf16[128,1024]{1,0:T(8,128)(2,1)S(1)}, bf16[128,1024]{1,0:T(8,128)(2,1)S(1)}, u32[]{:S(2)}, u32[]{:S(2)}) collective-permute-start(bf16[128,1024]{1,0:T(8,128)(2,1)S(1)} %depth.2.a_ref), channel_id=1, source_target_pairs={{0,4},{2,6},{4,0},{6,2},{1,5},{3,7},{5,1},{7,3},{8,12},{10,14},{12... | collective-permute-start | bytes 786440 | tf_op jit(solution)/shard_map/depth/ppermute | solution.py:39
  129.4 3.3 %all-to-all-start.4 = ((bf16[8,16,128]{2,1,0:T(8,128)(2,1)}), bf16[8,16,128]{2,1,0:T(8,128)(2,1)S(1)}, u32[]{:S(2)}, u32[]{:S(2)}) async-start(bf16[8,16,128]{2,1,0:T(8,128)(2,1)} %reshape.137), calls=%async_computation.4 | async-start | bytes 65536 | tf_op jit(solution)/shard_map/place_outputs/all_to_all | solution.py:27
  132.7 2.3 %collective-permute-done.14.b_ref = bf16[128,1024]{1,0:T(8,128)(2,1)S(1)} collective-permute-done((bf16[128,1024]{1,0:T(8,128)(2,1)S(1)}, bf16[128,1024]{1,0:T(8,128)(2,1)S(1)}, u32[]{:S(2)}, u32[]{:S(2)}) %collective-permute-start.14) | collective-permute-done | bytes 262176 | tf_op jit(solution)/shard_map/depth/ppermute | solution.py:39
  135.0 4.4 %collective-permute-done.15.c_ref = bf16[128,1024]{1,0:T(8,128)(2,1)S(1)} collective-permute-done((bf16[128,1024]{1,0:T(8,128)(2,1)S(1)}, bf16[128,1024]{1,0:T(8,128)(2,1)S(1)}, u32[]{:S(2)}, u32[]{:S(2)}) %collective-permute-start.15) | collective-permute-done | bytes 262176 | tf_op jit(solution)/shard_map/depth/ppermute | solution.py:39
  140.4 2.3 %copy-done.3 = bf16[2304,1024]{1,0:T(8,128)(2,1)S(1)} copy-done((bf16[2304,1024]{1,0:T(8,128)(2,1)S(1)}, bf16[2304,1024]{1,0:T(8,128)(2,1)}, u32[]{:S(2)}) %copy-start.3) | copy-done | bytes 4718616
  142.7 2.8 %depth.3 = bf16[8,4,32,128]{3,2,1,0:T(8,128)(2,1)} custom-call(bf16[128,1024]{1,0:T(8,128)(2,1)S(1)} %depth.2.a_ref, bf16[128,1024]{1,0:T(8,128)(2,1)S(1)} %collective-permute-done.14.b_ref, bf16[128,1024]{1,0:T(8,128)(2,1)S(1)} %collective-permute-done.15.c_ref, bf16[128,1024]{1,0:T(8,128)(2,1)S(1)} %collective-permute-done.16.d_ref, ...), custom_call_target="tpu_custom_call" | custom-call | flops 603979776 | bytes 5769216 | tf_op jit(solution)/shard_map/depth/pallas_call | solution.py:69
  145.5 6.2 %all-to-all-start.5 = ((bf16[64,16,128]{2,1,0:T(8,128)(2,1)}), bf16[64,16,128]{2,1,0:T(8,128)(2,1)S(1)}, u32[]{:S(2)}, u32[]{:S(2)}) async-start(bf16[64,16,128]{2,1,0:T(8,128)(2,1)} %bitcast.50), calls=%async_computation.5 | async-start | bytes 524288 | tf_op jit(solution)/shard_map/depth/all_to_all | solution.py:27
  152.6 12.3 %all-to-all-done.5 = bf16[64,16,128]{2,1,0:T(8,128)(2,1)S(1)} async-done(((bf16[64,16,128]{2,1,0:T(8,128)(2,1)}), bf16[64,16,128]{2,1,0:T(8,128)(2,1)S(1)}, u32[]{:S(2)}, u32[]{:S(2)}) %all-to-all-start.5) | async-done | bytes 262176 | tf_op jit(solution)/shard_map/depth/all_to_all | solution.py:27
  (137 shorter events, 30.9 us)
Async XLA Ops:
  7.2 72.1 %copy-start = (bf16[4,64,4096]{2,1,0:T(8,128)(2,1)S(1)}, bf16[4,64,4096]{2,1,0:T(8,128)(2,1)}, u32[]{:S(2)}) copy-start(bf16[4,64,4096]{2,1,0:T(8,128)(2,1)} %param.18) | copy-start | bytes 6291460
  7.2 68.4 %all-gather.5.cloned.1.call-start = ((), (), s32[]{:S(2)}) async-start(), calls=%async_computation.6 | async-start | bytes 3538944 | tf_op jit(solution)/shard_map/pack_weights/all_gather | solution.py:245
  8.4 4.3 %collective-permute-start.7 = (bf16[64,1024]{1,0:T(8,128)(2,1)S(1)}, bf16[64,1024]{1,0:T(8,128)(2,1)S(1)}, u32[]{:S(2)}, u32[]{:S(2)}) collective-permute-start(bf16[64,1024]{1,0:T(8,128)(2,1)S(1)} %get-tuple-element.39), channel_id=1, source_target_pairs={{0,1},{1,0},{2,3},{3,2},{4,5},{5,4},{6,7},{7,6},{8,9},{9,8},{10,11... | collective-permute-start | bytes 393224 | tf_op jit(solution)/shard_map/pack_weights/ppermute | solution.py:57
  13.5 115.8 %all-gather.7.cloned.1.call-start = ((), (), s32[]{:S(2)}) async-start(), calls=%async_computation.7 | async-start | bytes 5308416 | tf_op jit(solution)/shard_map/pack_weights/all_gather | solution.py:246
  13.9 1.7 collective-permute-start.11
  16.5 41.0 %collective-permute-start.6 = (bf16[192,4096]{1,0:T(8,128)(2,1)}, bf16[192,4096]{1,0:T(8,128)(2,1)}, u32[]{:S(2)}, u32[]{:S(2)}) collective-permute-start(bf16[192,4096]{1,0:T(8,128)(2,1)} %bitcast.103), channel_id=1, source_target_pairs={{0,1},{1,0},{2,3},{3,2},{4,5},{5,4},{6,7},{7,6},{8,9},{9,8},{10,11... | collective-permute-start | bytes 4718600 | tf_op jit(solution)/shard_map/norm/ppermute | solution.py:57
  41.6 6.5 %collective-permute-start = (bf16[528,128]{1,0:T(8,128)(2,1)S(1)}, bf16[528,128]{1,0:T(8,128)(2,1)S(1)}, u32[]{:S(2)}, u32[]{:S(2)}) collective-permute-start(bf16[528,128]{1,0:T(8,128)(2,1)S(1)} %fusion.21.refs_0_), channel_id=1, source_target_pairs={{0,2},{2,4},{4,6},{6,0},{1,3},{3,5},{5,7},{7,1},{8,10},{10,12},{12... | collective-permute-start | bytes 405512 | tf_op jit(solution)/shard_map/norm/ppermute | solution.py:47
  42.9 6.8 %collective-permute-start.3 = (bf16[512,128]{1,0:T(8,128)(2,1)S(1)}, bf16[512,128]{1,0:T(8,128)(2,1)S(1)}, u32[]{:S(2)}, u32[]{:S(2)}) collective-permute-start(bf16[512,128]{1,0:T(8,128)(2,1)S(1)} %bitcast.105), channel_id=1, source_target_pairs={{0,6},{2,0},{4,2},{6,4},{1,7},{3,1},{5,3},{7,5},{8,14},{10,8},{12,... | collective-permute-start | bytes 393224 | tf_op jit(solution)/shard_map/norm/ppermute | solution.py:48
  44.6 12.8 %collective-permute-start.2 = (bf16[528,128]{1,0:T(8,128)(2,1)S(1)}, bf16[528,128]{1,0:T(8,128)(2,1)S(1)}, u32[]{:S(2)}, u32[]{:S(2)}) collective-permute-start(bf16[528,128]{1,0:T(8,128)(2,1)S(1)} %fusion.21.refs_0_), channel_id=1, source_target_pairs={{0,6},{2,0},{4,2},{6,4},{1,7},{3,1},{5,3},{7,5},{8,14},{10,8},{12,... | collective-permute-start | bytes 405512 | tf_op jit(solution)/shard_map/norm/ppermute | solution.py:50
  48.1 9.4 %collective-permute-start.4 = (bf16[528,128]{1,0:T(8,128)(2,1)S(1)}, bf16[528,128]{1,0:T(8,128)(2,1)S(1)}, u32[]{:S(2)}, u32[]{:S(2)}) collective-permute-start(bf16[528,128]{1,0:T(8,128)(2,1)S(1)} %collective-permute-done.refs_2_), channel_id=1, source_target_pairs={{0,2},{2,4},{4,6},{6,0},{1,3},{3,5},{5,7},{7,1},{8,10},{10,12},{12... | collective-permute-start | bytes 405512 | tf_op jit(solution)/shard_map/norm/ppermute | solution.py:51
  48.3 9.2 %collective-permute-start.1 = (bf16[512,128]{1,0:T(8,128)(2,1)S(1)}, bf16[512,128]{1,0:T(8,128)(2,1)S(1)}, u32[]{:S(2)}, u32[]{:S(2)}) collective-permute-start(bf16[512,128]{1,0:T(8,128)(2,1)S(1)} %bitcast.106), channel_id=1, source_target_pairs={{0,2},{2,4},{4,6},{6,0},{1,3},{3,5},{5,7},{7,1},{8,10},{10,12},{12... | collective-permute-start | bytes 393224 | tf_op jit(solution)/shard_map/norm/ppermute | solution.py:49
  49.7 7.8 %collective-permute-start.5 = (bf16[512,128]{1,0:T(8,128)(2,1)S(1)}, bf16[512,128]{1,0:T(8,128)(2,1)S(1)}, u32[]{:S(2)}, u32[]{:S(2)}) collective-permute-start(bf16[512,128]{1,0:T(8,128)(2,1)S(1)} %collective-permute-done.3.refs_5_), channel_id=1, source_target_pairs={{0,6},{2,0},{4,2},{6,4},{1,7},{3,1},{5,3},{7,5},{8,14},{10,8},{12,... | collective-permute-start | bytes 393224 | tf_op jit(solution)/shard_map/norm/ppermute | solution.py:52
  62.2 13.3 %all-to-all-start.1 = ((bf16[32,4,512]{2,1,0:T(4,128)(2,1)}), bf16[32,4,512]{2,1,0:T(4,128)(2,1)S(1)}, u32[]{:S(2)}, u32[]{:S(2)}) async-start(bf16[32,4,512]{2,1,0:T(4,128)(2,1)} %reshape.130), calls=%async_computation.1 | async-start | bytes 262144 | tf_op jit(solution)/shard_map/qkv/all_to_all | solution.py:27
  99.2 10.2 %all-to-all-start.3 = ((bf16[8,128,128]{2,1,0:T(8,128)(2,1)}), bf16[8,128,128]{2,1,0:T(8,128)(2,1)S(1)}, u32[]{:S(2)}, u32[]{:S(2)}) async-start(bf16[8,128,128]{2,1,0:T(8,128)(2,1)} %project.1), calls=%async_computation.3 | async-start | bytes 524288 | tf_op jit(solution)/shard_map/project/all_to_all | solution.py:27
  109.5 4.8 %collective-permute-start.8 = (bf16[128,128]{1,0:T(8,128)(2,1)S(1)}, bf16[128,128]{1,0:T(8,128)(2,1)S(1)}, u32[]{:S(2)}, u32[]{:S(2)}) collective-permute-start(bf16[128,128]{1,0:T(8,128)(2,1)S(1)} %get-tuple-element.33), channel_id=1, source_target_pairs={{0,64},{64,128},{128,192},{192,0},{1,65},{65,129},{129,193},{193,1... | collective-permute-start | bytes 98312 | tf_op jit(solution)/shard_map/project/ppermute | solution.py:39
  110.7 11.3 %collective-permute-start.13 = (bf16[8,2,16,128]{3,2,1,0:T(8,128)(2,1)S(1)}, bf16[8,2,16,128]{3,2,1,0:T(8,128)(2,1)S(1)}, u32[]{:S(2)}, u32[]{:S(2)}) collective-permute-start(bf16[8,2,16,128]{3,2,1,0:T(8,128)(2,1)S(1)} %slice.87), channel_id=1, source_target_pairs={{0,64},{64,128},{128,192},{192,0},{1,1},{65,65},{129,129},{193,193... | collective-permute-start | bytes 196616 | tf_op jit(solution)/shard_map/embed/ppermute | solution.py:270
  111.4 4.4 %collective-permute-start.9 = (bf16[128,128]{1,0:T(8,128)(2,1)S(1)}, bf16[128,128]{1,0:T(8,128)(2,1)S(1)}, u32[]{:S(2)}, u32[]{:S(2)}) collective-permute-start(bf16[128,128]{1,0:T(8,128)(2,1)S(1)} %get-tuple-element.33), channel_id=1, source_target_pairs={{0,128},{64,192},{128,0},{192,64},{1,129},{65,193},{129,1},{193,65... | collective-permute-start | bytes 98312 | tf_op jit(solution)/shard_map/project/ppermute | solution.py:39
  113.2 3.3 %collective-permute-start.10 = (bf16[128,128]{1,0:T(8,128)(2,1)S(1)}, bf16[128,128]{1,0:T(8,128)(2,1)S(1)}, u32[]{:S(2)}, u32[]{:S(2)}) collective-permute-start(bf16[128,128]{1,0:T(8,128)(2,1)S(1)} %get-tuple-element.33), channel_id=1, source_target_pairs={{0,192},{64,0},{128,64},{192,128},{1,193},{65,1},{129,65},{193,129... | collective-permute-start | bytes 98312 | tf_op jit(solution)/shard_map/project/ppermute | solution.py:39
  116.5 6.5 %collective-permute-start.12 = (bf16[4,128,128]{2,1,0:T(8,128)(2,1)S(1)}, bf16[4,128,128]{2,1,0:T(8,128)(2,1)S(1)}, u32[]{:S(2)}, u32[]{:S(2)}) collective-permute-start(bf16[4,128,128]{2,1,0:T(8,128)(2,1)S(1)} %bitcast_dynamic-update-slice_fusion.own_ref), channel_id=1, source_target_pairs={{0,1},{1,0},{2,3},{3,2},{4,5},{5,4},{6,7},{7,6},{8,9},{9,8},{10,11... | collective-permute-start | bytes 393224 | tf_op jit(solution)/shard_map/project/ppermute | solution.py:57
  125.6 9.4 %collective-permute-start.14 = (bf16[128,1024]{1,0:T(8,128)(2,1)S(1)}, bf16[128,1024]{1,0:T(8,128)(2,1)S(1)}, u32[]{:S(2)}, u32[]{:S(2)}) collective-permute-start(bf16[128,1024]{1,0:T(8,128)(2,1)S(1)} %depth.2.a_ref), channel_id=1, source_target_pairs={{0,2},{2,4},{4,6},{6,0},{1,3},{3,5},{5,7},{7,1},{8,10},{10,12},{12... | collective-permute-start | bytes 786440 | tf_op jit(solution)/shard_map/depth/ppermute | solution.py:39
  126.0 13.5 %collective-permute-start.15 = (bf16[128,1024]{1,0:T(8,128)(2,1)S(1)}, bf16[128,1024]{1,0:T(8,128)(2,1)S(1)}, u32[]{:S(2)}, u32[]{:S(2)}) collective-permute-start(bf16[128,1024]{1,0:T(8,128)(2,1)S(1)} %depth.2.a_ref), channel_id=1, source_target_pairs={{0,4},{2,6},{4,0},{6,2},{1,5},{3,7},{5,1},{7,3},{8,12},{10,14},{12... | collective-permute-start | bytes 786440 | tf_op jit(solution)/shard_map/depth/ppermute | solution.py:39
  127.7 12.6 %collective-permute-start.16 = (bf16[128,1024]{1,0:T(8,128)(2,1)S(1)}, bf16[128,1024]{1,0:T(8,128)(2,1)S(1)}, u32[]{:S(2)}, u32[]{:S(2)}) collective-permute-start(bf16[128,1024]{1,0:T(8,128)(2,1)S(1)} %depth.2.a_ref), channel_id=1, source_target_pairs={{0,6},{2,0},{4,2},{6,4},{1,7},{3,1},{5,3},{7,5},{8,14},{10,8},{12,... | collective-permute-start | bytes 786440 | tf_op jit(solution)/shard_map/depth/ppermute | solution.py:39
  129.4 16.2 %all-to-all-start.4 = ((bf16[8,16,128]{2,1,0:T(8,128)(2,1)}), bf16[8,16,128]{2,1,0:T(8,128)(2,1)S(1)}, u32[]{:S(2)}, u32[]{:S(2)}) async-start(bf16[8,16,128]{2,1,0:T(8,128)(2,1)} %reshape.137), calls=%async_computation.4 | async-start | bytes 65536 | tf_op jit(solution)/shard_map/place_outputs/all_to_all | solution.py:27
  145.5 19.4 %all-to-all-start.5 = ((bf16[64,16,128]{2,1,0:T(8,128)(2,1)}), bf16[64,16,128]{2,1,0:T(8,128)(2,1)S(1)}, u32[]{:S(2)}, u32[]{:S(2)}) async-start(bf16[64,16,128]{2,1,0:T(8,128)(2,1)} %bitcast.50), calls=%async_computation.5 | async-start | bytes 524288 | tf_op jit(solution)/shard_map/depth/all_to_all | solution.py:27
  (14 other events, 65.1 us)
Sparse Core Ops, SparseCore 0:
  13.7 51.9 all-gather.4
  67.5 59.0 all-gather.6

commit v5 on v3

--- a/solution.py
+++ b/solution.py
@@ -151,7 +151,7 @@
     for i in range(4):
         acc += jnp.dot(
             moved_ref[:, i * 128 : (i + 1) * 128],
-            w_ref[2 * i : 2 * i + 2, 128:].reshape(128, DD),
+            w_ref[2 * i : 2 * i + 2].reshape(128, DD),
             preferred_element_type=F32,
         )
     for block in range(8):
@@ -275,7 +275,7 @@
         emb = jnp.dot(emb.T, place, preferred_element_type=F32).astype(BF)
 
     with jax.named_scope("attend"):
-        got, first = lax.optimization_barrier((got, first))
+        got, first, wo_all = lax.optimization_barrier((got, first, first[:, 128:]))
         query_h, key_new, value_new = got[:, 0], got[:, 1], got[:, 2]
         hid_rows = got[:, 3]
         scale = 1.0 / math.sqrt(HEAD_DIM)
@@ -303,7 +303,7 @@
         moved = exchange(
             jnp.concatenate([att, res], axis=-1).reshape(32, 4, 640), ("cb", "y", "core")
         ).reshape(128, 640)
-        part = in_vmem(project_kernel, (8, 128, 128), 2 * 128 * 512 * DD, (moved[:, :512], first))
+        part = in_vmem(project_kernel, (8, 128, 128), 2 * 128 * 512 * DD, (moved[:, :512], wo_all))
         part = exchange(part, ("y", "core"))
         temporal = jnp.sum(part.astype(F32), axis=0) + moved[:, 512:].astype(F32)
         temporal = temporal.astype(BF)

time: 169 us -> 169 us (level)
  starting transfers between devices: 41.3 us -> 43 us
where the time goes in v5:
time: 169 us; the launch traced here: 168 us
  waiting for transfers between devices  44 us (26%)
  starting transfers between devices  43 us (25%)
  blocking collectives  39.1 us (23%)
  between operations  14.7 us (9%)
  local copies, waits for them, and re-layouts  14.3 us (8%)
  Pallas kernels  7.85 us (5%)
  other arithmetic  3.17 us (2%)
  matrix products  2.28 us (1%)
    all_to_all x2, blocking collectives, exchange(): return lax.all_to_all(value, axis, split_axis=0, concat_axis=0, tiled=True)  39.1 us
    all_to_all x4, waiting for transfers between devices, exchange(): return lax.all_to_all(value, axis, split_axis=0, concat_axis=0, tiled=True)  26.7 us
    all_to_all x4, starting transfers between devices, exchange(): return lax.all_to_all(value, axis, split_axis=0, concat_axis=0, tiled=True)  19.8 us
    ppermute x6, starting transfers between devices, from_each(): lax.ppermute(value, axis, [(i, (i + step) % count) for i in range(count)])  8.3 us
    pallas_call x4, Pallas kernels, in_vmem(): pl.pallas_call(kernel, in_specs=[pl.BlockSpec(memory_space=pltpu.VMEM)] *...  7.29 us
    ppermute x4, starting transfers between devices, swap(): return lax.ppermute(value, 'core', [(0, 1), (1, 0)])  6.38 us
    ppermute x1, waiting for transfers between devices, ring_halves(): high_behind = lax.ppermute(high, axis, up)  5.97 us
    unnamed x36, local copies, waits for them, and re-layouts  5.75 us
  transfers between devices with their start and end apart: 23, of which 13 were waited for; matrix products, arithmetic and copies ran while one was open for 7% of the time, Pallas kernels for 5%

profile of v5, /device:TPU:1, one launch (start us, length us, event | category | flops | bytes accessed | tf_op | source)
XLA Modules:
  0.0 168.4 jit_solution(3364674424924224533)
XLA Ops:
  8.4 3.3 %collective-permute-start.7 = (bf16[64,1024]{1,0:T(8,128)(2,1)S(1)}, bf16[64,1024]{1,0:T(8,128)(2,1)S(1)}, u32[]{:S(2)}, u32[]{:S(2)}) collective-permute-start(bf16[64,1024]{1,0:T(8,128)(2,1)S(1)} %get-tuple-element.41), channel_id=1, source_target_pairs={{0,1},{1,0},{2,3},{3,2},{4,5},{5,4},{6,7},{7,6},{8,9},{9,8},{10,11... | collective-permute-start | bytes 393224 | tf_op jit(solution)/shard_map/pack_weights/ppermute | solution.py:57
  17.7 23.8 %all_to_all.30 = bf16[16,88,128]{2,1,0:T(8,128)(2,1)S(1)} all-to-all(bf16[16,88,128]{2,1,0:T(8,128)(2,1)S(1)} %bitcast.119), channel_id=1, replica_groups=mesh['cb'=4,'z'=8,'y'=4,'core'=2] {'z','core'}, dimensions={0} | all-to-all | bytes 720896 | tf_op jit(solution)/shard_map/gather_hidden/all_to_all | solution.py:27
  42.9 1.7 collective-permute-start.3
  46.0 2.1 %collective-permute-done.refs_2_ = bf16[528,128]{1,0:T(8,128)(2,1)S(1)} collective-permute-done((bf16[528,128]{1,0:T(8,128)(2,1)S(1)}, bf16[528,128]{1,0:T(8,128)(2,1)S(1)}, u32[]{:S(2)}, u32[]{:S(2)}) %collective-permute-start) | collective-permute-done | bytes 135200 | tf_op jit(solution)/shard_map/norm/ppermute | solution.py:47
  49.7 1.8 %collective-permute-start.5 = (bf16[512,128]{1,0:T(8,128)(2,1)S(1)}, bf16[512,128]{1,0:T(8,128)(2,1)S(1)}, u32[]{:S(2)}, u32[]{:S(2)}) collective-permute-start(bf16[512,128]{1,0:T(8,128)(2,1)S(1)} %collective-permute-done.3.refs_5_), channel_id=1, source_target_pairs={{0,6},{2,0},{4,2},{6,4},{1,7},{3,1},{5,3},{7,5},{8,14},{10,8},{12,... | collective-permute-start | bytes 393224 | tf_op jit(solution)/shard_map/norm/ppermute | solution.py:52
  51.5 6.0 %collective-permute-done.1.refs_3_ = bf16[512,128]{1,0:T(8,128)(2,1)S(1)} collective-permute-done((bf16[512,128]{1,0:T(8,128)(2,1)S(1)}, bf16[512,128]{1,0:T(8,128)(2,1)S(1)}, u32[]{:S(2)}, u32[]{:S(2)}) %collective-permute-start.1) | collective-permute-done | bytes 131104 | tf_op jit(solution)/shard_map/norm/ppermute | solution.py:49
  58.9 2.6 %qkv.1 = bf16[128,512]{1,0:T(8,128)(2,1)S(1)} custom-call(bf16[528,128]{1,0:T(8,128)(2,1)S(1)} %fusion.21.refs_0_, bf16[512,128]{1,0:T(8,128)(2,1)S(1)} %bitcast.107, bf16[528,128]{1,0:T(8,128)(2,1)S(1)} %collective-permute-done.refs_2_, bf16[512,128]{1,0:T(8,128)(2,1)S(1)} %collective-permute-done.1.refs_3_, ...), custom_call_target="tpu_custom_call" | custom-call | flops 402653184 | bytes 4243456 | tf_op jit(solution)/shard_map/qkv/pallas_call | solution.py:69
  62.2 3.8 %all-to-all-start.1 = ((bf16[32,4,512]{2,1,0:T(4,128)(2,1)}), bf16[32,4,512]{2,1,0:T(4,128)(2,1)S(1)}, u32[]{:S(2)}, u32[]{:S(2)}) async-start(bf16[32,4,512]{2,1,0:T(4,128)(2,1)} %reshape.130), calls=%async_computation.1 | async-start | bytes 262144 | tf_op jit(solution)/shard_map/qkv/all_to_all | solution.py:27
  66.1 9.3 %all-to-all-done.1 = bf16[32,4,512]{2,1,0:T(4,128)(2,1)S(1)} async-done(((bf16[32,4,512]{2,1,0:T(4,128)(2,1)}), bf16[32,4,512]{2,1,0:T(4,128)(2,1)S(1)}, u32[]{:S(2)}, u32[]{:S(2)}) %all-to-all-start.1) | async-done | bytes 131104 | tf_op jit(solution)/shard_map/qkv/all_to_all | solution.py:27
  75.6 1.5 slice.81.w_ref
  80.9 15.3 %all_to_all.31 = bf16[32,4,640]{2,1,0:T(4,128)(2,1)S(1)} all-to-all(bf16[32,4,640]{2,1,0:T(4,128)(2,1)S(1)} %pad_maximum_fusion.2), channel_id=1, replica_groups=mesh['cb'=4,'z'=8,'y'=4,'core'=2] {'cb','y','core'}, dimensions={0} | all-to-all | bytes 327680 | tf_op jit(solution)/shard_map/project/all_to_all | solution.py:27
  97.5 3.7 %all-to-all-start.3 = ((bf16[8,128,128]{2,1,0:T(8,128)(2,1)}), bf16[8,128,128]{2,1,0:T(8,128)(2,1)S(1)}, u32[]{:S(2)}, u32[]{:S(2)}) async-start(bf16[8,128,128]{2,1,0:T(8,128)(2,1)} %project.1), calls=%async_computation.3 | async-start | bytes 524288 | tf_op jit(solution)/shard_map/project/all_to_all | solution.py:27
  102.8 5.0 %all-to-all-done.3 = bf16[8,128,128]{2,1,0:T(8,128)(2,1)S(1)} async-done(((bf16[8,128,128]{2,1,0:T(8,128)(2,1)}), bf16[8,128,128]{2,1,0:T(8,128)(2,1)S(1)}, u32[]{:S(2)}, u32[]{:S(2)}) %all-to-all-start.3) | async-done | bytes 262176 | tf_op jit(solution)/shard_map/project/all_to_all | solution.py:27
  109.3 1.5 collective-permute-start.9
  114.2 2.2 %collective-permute-start.12 = (bf16[4,128,128]{2,1,0:T(8,128)(2,1)S(1)}, bf16[4,128,128]{2,1,0:T(8,128)(2,1)S(1)}, u32[]{:S(2)}, u32[]{:S(2)}) collective-permute-start(bf16[4,128,128]{2,1,0:T(8,128)(2,1)S(1)} %bitcast_dynamic-update-slice_fusion.own_ref), channel_id=1, source_target_pairs={{0,1},{1,0},{2,3},{3,2},{4,5},{5,4},{6,7},{7,6},{8,9},{9,8},{10,11... | collective-permute-start | bytes 393224 | tf_op jit(solution)/shard_map/project/ppermute | solution.py:57
  118.0 1.4 collective-permute-start.14
  119.5 2.4 %collective-permute-start.15 = (bf16[128,1024]{1,0:T(8,128)(2,1)S(1)}, bf16[128,1024]{1,0:T(8,128)(2,1)S(1)}, u32[]{:S(2)}, u32[]{:S(2)}) collective-permute-start(bf16[128,1024]{1,0:T(8,128)(2,1)S(1)} %depth.2.a_ref), channel_id=1, source_target_pairs={{0,4},{2,6},{4,0},{6,2},{1,5},{3,7},{5,1},{7,3},{8,12},{10,14},{12... | collective-permute-start | bytes 786440 | tf_op jit(solution)/shard_map/depth/ppermute | solution.py:39
  123.9 2.6 %all-gather.7.cloned.1.call-done = bf16[2304,1024]{1,0:T(8,128)(2,1)} async-done(((bf16[288,1024]{1,0:T(8,128)(2,1)}), bf16[2304,1024]{1,0:T(8,128)(2,1)}) %all-gather.7.cloned.1.call-update) | async-done | bytes 4718608 | tf_op jit(solution)/shard_map/pack_weights/all_gather | solution.py:246
  126.6 4.0 %all-to-all-start.4 = ((bf16[8,16,128]{2,1,0:T(8,128)(2,1)}), bf16[8,16,128]{2,1,0:T(8,128)(2,1)S(1)}, u32[]{:S(2)}, u32[]{:S(2)}) async-start(bf16[8,16,128]{2,1,0:T(8,128)(2,1)} %reshape.137), calls=%async_computation.4 | async-start | bytes 65536 | tf_op jit(solution)/shard_map/place_outputs/all_to_all | solution.py:27
  130.6 2.9 %collective-permute-done.15.c_ref = bf16[128,1024]{1,0:T(8,128)(2,1)S(1)} collective-permute-done((bf16[128,1024]{1,0:T(8,128)(2,1)S(1)}, bf16[128,1024]{1,0:T(8,128)(2,1)S(1)}, u32[]{:S(2)}, u32[]{:S(2)}) %collective-permute-start.15) | collective-permute-done | bytes 262176 | tf_op jit(solution)/shard_map/depth/ppermute | solution.py:39
  133.6 2.3 %copy-done.2 = bf16[2304,1024]{1,0:T(8,128)(2,1)S(1)} copy-done((bf16[2304,1024]{1,0:T(8,128)(2,1)S(1)}, bf16[2304,1024]{1,0:T(8,128)(2,1)}, u32[]{:S(2)}) %copy-start.2) | copy-done | bytes 4718616
  135.9 2.8 %depth.3 = bf16[8,4,32,128]{3,2,1,0:T(8,128)(2,1)} custom-call(bf16[128,1024]{1,0:T(8,128)(2,1)S(1)} %depth.2.a_ref, bf16[128,1024]{1,0:T(8,128)(2,1)S(1)} %collective-permute-done.14.b_ref, bf16[128,1024]{1,0:T(8,128)(2,1)S(1)} %collective-permute-done.15.c_ref, bf16[128,1024]{1,0:T(8,128)(2,1)S(1)} %collective-permute-done.16.d_ref, ...), custom_call_target="tpu_custom_call" | custom-call | flops 603979776 | bytes 5769216 | tf_op jit(solution)/shard_map/depth/pallas_call | solution.py:69
  138.7 8.2 %all-to-all-start.5 = ((bf16[64,16,128]{2,1,0:T(8,128)(2,1)}), bf16[64,16,128]{2,1,0:T(8,128)(2,1)S(1)}, u32[]{:S(2)}, u32[]{:S(2)}) async-start(bf16[64,16,128]{2,1,0:T(8,128)(2,1)} %bitcast.50), calls=%async_computation.5 | async-start | bytes 524288 | tf_op jit(solution)/shard_map/depth/all_to_all | solution.py:27
  147.8 12.3 %all-to-all-done.5 = bf16[64,16,128]{2,1,0:T(8,128)(2,1)S(1)} async-done(((bf16[64,16,128]{2,1,0:T(8,128)(2,1)}), bf16[64,16,128]{2,1,0:T(8,128)(2,1)S(1)}, u32[]{:S(2)}, u32[]{:S(2)}) %all-to-all-start.5) | async-done | bytes 262176 | tf_op jit(solution)/shard_map/depth/all_to_all | solution.py:27
  (139 shorter events, 31.0 us)
Async XLA Ops:
  7.2 72.4 %copy-start = (bf16[4,64,4096]{2,1,0:T(8,128)(2,1)S(1)}, bf16[4,64,4096]{2,1,0:T(8,128)(2,1)}, u32[]{:S(2)}) copy-start(bf16[4,64,4096]{2,1,0:T(8,128)(2,1)} %param.18) | copy-start | bytes 6291460
  7.2 68.4 %all-gather.5.cloned.1.call-start = ((), (), s32[]{:S(2)}) async-start(), calls=%async_computation.6 | async-start | bytes 3538944 | tf_op jit(solution)/shard_map/pack_weights/all_gather | solution.py:245
  8.4 4.3 %collective-permute-start.7 = (bf16[64,1024]{1,0:T(8,128)(2,1)S(1)}, bf16[64,1024]{1,0:T(8,128)(2,1)S(1)}, u32[]{:S(2)}, u32[]{:S(2)}) collective-permute-start(bf16[64,1024]{1,0:T(8,128)(2,1)S(1)} %get-tuple-element.41), channel_id=1, source_target_pairs={{0,1},{1,0},{2,3},{3,2},{4,5},{5,4},{6,7},{7,6},{8,9},{9,8},{10,11... | collective-permute-start | bytes 393224 | tf_op jit(solution)/shard_map/pack_weights/ppermute | solution.py:57
  13.5 113.0 %all-gather.7.cloned.1.call-start = ((), (), s32[]{:S(2)}) async-start(), calls=%async_computation.7 | async-start | bytes 5308416 | tf_op jit(solution)/shard_map/pack_weights/all_gather | solution.py:246
  13.9 1.7 collective-permute-start.11
  16.5 41.0 %collective-permute-start.6 = (bf16[192,4096]{1,0:T(8,128)(2,1)}, bf16[192,4096]{1,0:T(8,128)(2,1)}, u32[]{:S(2)}, u32[]{:S(2)}) collective-permute-start(bf16[192,4096]{1,0:T(8,128)(2,1)} %bitcast.103), channel_id=1, source_target_pairs={{0,1},{1,0},{2,3},{3,2},{4,5},{5,4},{6,7},{7,6},{8,9},{9,8},{10,11... | collective-permute-start | bytes 4718600 | tf_op jit(solution)/shard_map/norm/ppermute | solution.py:57
  41.6 6.5 %collective-permute-start = (bf16[528,128]{1,0:T(8,128)(2,1)S(1)}, bf16[528,128]{1,0:T(8,128)(2,1)S(1)}, u32[]{:S(2)}, u32[]{:S(2)}) collective-permute-start(bf16[528,128]{1,0:T(8,128)(2,1)S(1)} %fusion.21.refs_0_), channel_id=1, source_target_pairs={{0,2},{2,4},{4,6},{6,0},{1,3},{3,5},{5,7},{7,1},{8,10},{10,12},{12... | collective-permute-start | bytes 405512 | tf_op jit(solution)/shard_map/norm/ppermute | solution.py:47
  42.9 6.8 %collective-permute-start.3 = (bf16[512,128]{1,0:T(8,128)(2,1)S(1)}, bf16[512,128]{1,0:T(8,128)(2,1)S(1)}, u32[]{:S(2)}, u32[]{:S(2)}) collective-permute-start(bf16[512,128]{1,0:T(8,128)(2,1)S(1)} %bitcast.105), channel_id=1, source_target_pairs={{0,6},{2,0},{4,2},{6,4},{1,7},{3,1},{5,3},{7,5},{8,14},{10,8},{12,... | collective-permute-start | bytes 393224 | tf_op jit(solution)/shard_map/norm/ppermute | solution.py:48
  44.6 12.8 %collective-permute-start.2 = (bf16[528,128]{1,0:T(8,128)(2,1)S(1)}, bf16[528,128]{1,0:T(8,128)(2,1)S(1)}, u32[]{:S(2)}, u32[]{:S(2)}) collective-permute-start(bf16[528,128]{1,0:T(8,128)(2,1)S(1)} %fusion.21.refs_0_), channel_id=1, source_target_pairs={{0,6},{2,0},{4,2},{6,4},{1,7},{3,1},{5,3},{7,5},{8,14},{10,8},{12,... | collective-permute-start | bytes 405512 | tf_op jit(solution)/shard_map/norm/ppermute | solution.py:50
  48.1 9.4 %collective-permute-start.4 = (bf16[528,128]{1,0:T(8,128)(2,1)S(1)}, bf16[528,128]{1,0:T(8,128)(2,1)S(1)}, u32[]{:S(2)}, u32[]{:S(2)}) collective-permute-start(bf16[528,128]{1,0:T(8,128)(2,1)S(1)} %collective-permute-done.refs_2_), channel_id=1, source_target_pairs={{0,2},{2,4},{4,6},{6,0},{1,3},{3,5},{5,7},{7,1},{8,10},{10,12},{12... | collective-permute-start | bytes 405512 | tf_op jit(solution)/shard_map/norm/ppermute | solution.py:51
  48.3 9.2 %collective-permute-start.1 = (bf16[512,128]{1,0:T(8,128)(2,1)S(1)}, bf16[512,128]{1,0:T(8,128)(2,1)S(1)}, u32[]{:S(2)}, u32[]{:S(2)}) collective-permute-start(bf16[512,128]{1,0:T(8,128)(2,1)S(1)} %bitcast.106), channel_id=1, source_target_pairs={{0,2},{2,4},{4,6},{6,0},{1,3},{3,5},{5,7},{7,1},{8,10},{10,12},{12... | collective-permute-start | bytes 393224 | tf_op jit(solution)/shard_map/norm/ppermute | solution.py:49
  49.7 7.8 %collective-permute-start.5 = (bf16[512,128]{1,0:T(8,128)(2,1)S(1)}, bf16[512,128]{1,0:T(8,128)(2,1)S(1)}, u32[]{:S(2)}, u32[]{:S(2)}) collective-permute-start(bf16[512,128]{1,0:T(8,128)(2,1)S(1)} %collective-permute-done.3.refs_5_), channel_id=1, source_target_pairs={{0,6},{2,0},{4,2},{6,4},{1,7},{3,1},{5,3},{7,5},{8,14},{10,8},{12,... | collective-permute-start | bytes 393224 | tf_op jit(solution)/shard_map/norm/ppermute | solution.py:52
  62.2 13.3 %all-to-all-start.1 = ((bf16[32,4,512]{2,1,0:T(4,128)(2,1)}), bf16[32,4,512]{2,1,0:T(4,128)(2,1)S(1)}, u32[]{:S(2)}, u32[]{:S(2)}) async-start(bf16[32,4,512]{2,1,0:T(4,128)(2,1)} %reshape.130), calls=%async_computation.1 | async-start | bytes 262144 | tf_op jit(solution)/shard_map/qkv/all_to_all | solution.py:27
  97.5 10.2 %all-to-all-start.3 = ((bf16[8,128,128]{2,1,0:T(8,128)(2,1)}), bf16[8,128,128]{2,1,0:T(8,128)(2,1)S(1)}, u32[]{:S(2)}, u32[]{:S(2)}) async-start(bf16[8,128,128]{2,1,0:T(8,128)(2,1)} %project.1), calls=%async_computation.3 | async-start | bytes 524288 | tf_op jit(solution)/shard_map/project/all_to_all | solution.py:27
  102.1 6.1 %collective-permute-start.13 = (bf16[8,2,16,128]{3,2,1,0:T(8,128)(2,1)S(1)}, bf16[8,2,16,128]{3,2,1,0:T(8,128)(2,1)S(1)}, u32[]{:S(2)}, u32[]{:S(2)}) collective-permute-start(bf16[8,2,16,128]{3,2,1,0:T(8,128)(2,1)S(1)} %slice.92), channel_id=1, source_target_pairs={{0,64},{64,128},{128,192},{192,0},{2,66},{66,130},{130,194},{194,2... | collective-permute-start | bytes 196616 | tf_op jit(solution)/shard_map/embed/ppermute | solution.py:268
  107.9 4.5 %collective-permute-start.8 = (bf16[128,128]{1,0:T(8,128)(2,1)S(1)}, bf16[128,128]{1,0:T(8,128)(2,1)S(1)}, u32[]{:S(2)}, u32[]{:S(2)}) collective-permute-start(bf16[128,128]{1,0:T(8,128)(2,1)S(1)} %get-tuple-element.35), channel_id=1, source_target_pairs={{0,64},{64,128},{128,192},{192,0},{1,65},{65,129},{129,193},{193,1... | collective-permute-start | bytes 98312 | tf_op jit(solution)/shard_map/project/ppermute | solution.py:39
  109.3 4.4 %collective-permute-start.9 = (bf16[128,128]{1,0:T(8,128)(2,1)S(1)}, bf16[128,128]{1,0:T(8,128)(2,1)S(1)}, u32[]{:S(2)}, u32[]{:S(2)}) collective-permute-start(bf16[128,128]{1,0:T(8,128)(2,1)S(1)} %get-tuple-element.35), channel_id=1, source_target_pairs={{0,128},{64,192},{128,0},{192,64},{1,129},{65,193},{129,1},{193,65... | collective-permute-start | bytes 98312 | tf_op jit(solution)/shard_map/project/ppermute | solution.py:39
  110.9 3.3 %collective-permute-start.10 = (bf16[128,128]{1,0:T(8,128)(2,1)S(1)}, bf16[128,128]{1,0:T(8,128)(2,1)S(1)}, u32[]{:S(2)}, u32[]{:S(2)}) collective-permute-start(bf16[128,128]{1,0:T(8,128)(2,1)S(1)} %get-tuple-element.35), channel_id=1, source_target_pairs={{0,192},{64,0},{128,64},{192,128},{1,193},{65,1},{129,65},{193,129... | collective-permute-start | bytes 98312 | tf_op jit(solution)/shard_map/project/ppermute | solution.py:39
  114.2 3.1 %collective-permute-start.12 = (bf16[4,128,128]{2,1,0:T(8,128)(2,1)S(1)}, bf16[4,128,128]{2,1,0:T(8,128)(2,1)S(1)}, u32[]{:S(2)}, u32[]{:S(2)}) collective-permute-start(bf16[4,128,128]{2,1,0:T(8,128)(2,1)S(1)} %bitcast_dynamic-update-slice_fusion.own_ref), channel_id=1, source_target_pairs={{0,1},{1,0},{2,3},{3,2},{4,5},{5,4},{6,7},{7,6},{8,9},{9,8},{10,11... | collective-permute-start | bytes 393224 | tf_op jit(solution)/shard_map/project/ppermute | solution.py:57
  118.0 12.6 %collective-permute-start.14 = (bf16[128,1024]{1,0:T(8,128)(2,1)S(1)}, bf16[128,1024]{1,0:T(8,128)(2,1)S(1)}, u32[]{:S(2)}, u32[]{:S(2)}) collective-permute-start(bf16[128,1024]{1,0:T(8,128)(2,1)S(1)} %depth.2.a_ref), channel_id=1, source_target_pairs={{0,2},{2,4},{4,6},{6,0},{1,3},{3,5},{5,7},{7,1},{8,10},{10,12},{12... | collective-permute-start | bytes 786440 | tf_op jit(solution)/shard_map/depth/ppermute | solution.py:39
  119.5 14.1 %collective-permute-start.15 = (bf16[128,1024]{1,0:T(8,128)(2,1)S(1)}, bf16[128,1024]{1,0:T(8,128)(2,1)S(1)}, u32[]{:S(2)}, u32[]{:S(2)}) collective-permute-start(bf16[128,1024]{1,0:T(8,128)(2,1)S(1)} %depth.2.a_ref), channel_id=1, source_target_pairs={{0,4},{2,6},{4,0},{6,2},{1,5},{3,7},{5,1},{7,3},{8,12},{10,14},{12... | collective-permute-start | bytes 786440 | tf_op jit(solution)/shard_map/depth/ppermute | solution.py:39
  121.9 11.7 %collective-permute-start.16 = (bf16[128,1024]{1,0:T(8,128)(2,1)S(1)}, bf16[128,1024]{1,0:T(8,128)(2,1)S(1)}, u32[]{:S(2)}, u32[]{:S(2)}) collective-permute-start(bf16[128,1024]{1,0:T(8,128)(2,1)S(1)} %depth.2.a_ref), channel_id=1, source_target_pairs={{0,6},{2,0},{4,2},{6,4},{1,7},{3,1},{5,3},{7,5},{8,14},{10,8},{12,... | collective-permute-start | bytes 786440 | tf_op jit(solution)/shard_map/depth/ppermute | solution.py:39
  126.6 12.1 %all-to-all-start.4 = ((bf16[8,16,128]{2,1,0:T(8,128)(2,1)}), bf16[8,16,128]{2,1,0:T(8,128)(2,1)S(1)}, u32[]{:S(2)}, u32[]{:S(2)}) async-start(bf16[8,16,128]{2,1,0:T(8,128)(2,1)} %reshape.137), calls=%async_computation.4 | async-start | bytes 65536 | tf_op jit(solution)/shard_map/place_outputs/all_to_all | solution.py:27
  138.7 21.4 %all-to-all-start.5 = ((bf16[64,16,128]{2,1,0:T(8,128)(2,1)}), bf16[64,16,128]{2,1,0:T(8,128)(2,1)S(1)}, u32[]{:S(2)}, u32[]{:S(2)}) async-start(bf16[64,16,128]{2,1,0:T(8,128)(2,1)} %bitcast.50), calls=%async_computation.5 | async-start | bytes 524288 | tf_op jit(solution)/shard_map/depth/all_to_all | solution.py:27
  (14 other events, 78.8 us)
Sparse Core Ops, SparseCore 0:
  13.7 51.9 all-gather.4
  67.5 59.0 all-gather.6
